TPU v7x, 128 devices: a whole 4x4x4 slice. The times are simulated.
128 devices in a mesh: gz: 8 (over x, z_hi), gy: 4 (over z_lo, core), gx: 4 (over y).
Axes of the slice: x: 4, y: 4, z: 4 (z_hi: 2, z_lo: 2; z = z_hi * 2 + z_lo), core: 2. Of those that a mesh axis runs over, the one named last changes fastest.
Arguments:
- coeff_z: float32 [128, 128, 512], P('gz', 'gy', 'gx'), may hold values from 0.2 to 5
- coeff_y: float32 [128, 128, 512], P('gz', 'gy', 'gx'), may hold values from 0.2 to 5
- coeff_x: float32 [128, 128, 512], P('gz', 'gy', 'gx'), may hold values from 0.2 to 5
- reaction: float32 [128, 128, 512], P('gz', 'gy', 'gx'), may hold values from 0.1 to 2
Outputs:
- level_one: float32 [27, 64, 64, 256], P(None, 'gz', 'gy', 'gx')
- level_two: float32 [27, 32, 32, 128], P(None, 'gz', 'gy', 'gx')
- level_three: float32 [27, 16, 16, 64], P(None, 'gz')
All inputs are finite; a program needn't handle non-finite values.
Results may differ from a plain program's by a relative error of at most 0.0003.
Values sent between devices are 32-bit elements; how exact they have to be, the bound alone decides.
A program may use at most 128 MiB of HBM per device.

v0:
```python
from functools import partial

import jax
import jax.numpy as jnp
from jax import lax
from jax.sharding import PartitionSpec as P


def shifted(block, axis, distance):
    devices = range(lax.axis_size(axis))
    route = [(i - distance, i) for i in devices if i - distance in devices]
    return lax.ppermute(block, axis, route)


def with_halo(block, sides, width):
    for axis, dim in sides:
        count = lax.axis_size(axis)
        forward = [(i, i + 1) for i in range(count - 1)]
        backward = [(target, source) for source, target in forward]
        low = lax.ppermute(
            lax.slice_in_dim(block, block.shape[dim] - width, None, axis=dim), axis, forward
        )
        high = lax.ppermute(lax.slice_in_dim(block, 0, width, axis=dim), axis, backward)
        block = jnp.concatenate([low, block, high], axis=dim)
    return block


def probe_lines(start, count, nfine, palette):
    places = start + jnp.arange(count, dtype=jnp.int32)
    ncoarse = nfine // 2

    def coarse_value(index):
        inside = (index >= 0) & (index < ncoarse)
        match = jnp.mod(index[None, :], 3) == palette[:, None]
        return jnp.where(match & inside[None, :], 1.0, 0.0).astype(jnp.float32)

    halves = jnp.floor_divide(places, 2)
    at_odd = coarse_value(halves)
    at_even = 0.5 * (coarse_value(halves - 1) + at_odd)
    value = jnp.where((jnp.mod(places, 2) == 1)[None, :], at_odd, at_even)
    return jnp.where(((places >= 0) & (places < nfine))[None, :], value, 0.0)


def select_lines(probe_sets, colours):
    match = colours[:, None] == jnp.arange(3, dtype=jnp.int32)[None, :]
    return jnp.sum(jnp.where(match[:, :, None], probe_sets[None, :, :], 0.0), axis=1)


def restrict_axis(field, axis):
    length = field.shape[axis] - 1
    lower = lax.slice_in_dim(field, 0, length, 2, axis)
    middle = lax.slice_in_dim(field, 1, length + 1, 2, axis)
    upper = lax.slice_in_dim(field, 2, length + 1, 2, axis)
    return 0.5 * lower + middle + 0.5 * upper


def window(block, lows, count):
    return lax.slice(
        block,
        (0, lows[0], lows[1], lows[2]),
        (block.shape[0], lows[0] + count[0] + 1, lows[1] + count[1] + 1, lows[2] + count[2] + 1),
    )


def fine_apply(padded, field, count):
    centre = window(field, (1, 1, 1), count)
    image = window(padded[3:4], (1, 1, 1), count) * centre
    image = image + window(padded[0:1], (1, 1, 1), count) * (
        centre - window(field, (2, 1, 1), count)
    )
    image = image + window(padded[0:1], (0, 1, 1), count) * (
        centre - window(field, (0, 1, 1), count)
    )
    image = image + window(padded[1:2], (1, 1, 1), count) * (
        centre - window(field, (1, 2, 1), count)
    )
    image = image + window(padded[1:2], (1, 0, 1), count) * (
        centre - window(field, (1, 0, 1), count)
    )
    image = image + window(padded[2:3], (1, 1, 1), count) * (
        centre - window(field, (1, 1, 2), count)
    )
    image = image + window(padded[2:3], (1, 1, 0), count) * (
        centre - window(field, (1, 1, 0), count)
    )
    return image


def stencil_apply(padded, field, count):
    image = jnp.zeros((field.shape[0], count[0] + 1, count[1] + 1, count[2] + 1), jnp.float32)
    for offset in range(27):
        shift_z = offset // 9 - 1
        shift_y = offset // 3 % 3 - 1
        shift_x = offset % 3 - 1
        image = image + window(padded[offset : offset + 1], (1, 1, 1), count) * window(
            field, (1 + shift_z, 1 + shift_y, 1 + shift_x), count
        )
    return image


def galerkin(apply_fn, starts, count, totals, group):
    palette = jnp.arange(3, dtype=jnp.int32)
    probe_sets = [
        probe_lines(starts[axis] - 1, count[axis] + 3, totals[axis], palette) for axis in range(3)
    ]
    limits = [
        starts[axis] + jnp.arange(count[axis] + 1, dtype=jnp.int32) < totals[axis]
        for axis in range(3)
    ]
    inside = limits[0][:, None, None] & limits[1][None, :, None] & limits[2][None, None, :]

    def colour_block(number):
        colours = number * group + jnp.arange(group, dtype=jnp.int32)
        line_z = select_lines(probe_sets[0], colours // 9)
        line_y = select_lines(probe_sets[1], colours // 3 % 3)
        line_x = select_lines(probe_sets[2], colours % 3)
        field = line_z[:, :, None, None] * line_y[:, None, :, None] * line_x[:, None, None, :]
        image = jnp.where(inside[None], apply_fn(field, count), 0.0)
        return 0.5 * restrict_axis(restrict_axis(restrict_axis(image, 1), 2), 3)

    blocks = lax.map(colour_block, jnp.arange(27 // group, dtype=jnp.int32))
    coarse_shape = blocks.shape[2:]
    products = blocks.reshape((3, 3, 3) + coarse_shape)
    choosers = []
    for axis in range(3):
        coarse = starts[axis] // 2 + jnp.arange(count[axis] // 2, dtype=jnp.int32)
        wanted = jnp.mod(coarse[None, :] + palette[:, None] - 1, 3)
        choosers.append(
            jnp.where(wanted[:, None, :] == palette[None, :, None], 1.0, 0.0).astype(jnp.float32)
        )
    first_pass = jnp.sum(choosers[0][:, :, None, None, :, None, None] * products[None], axis=1)
    second_pass = jnp.sum(
        choosers[1][None, :, :, None, None, :, None] * first_pass[:, None], axis=2
    )
    third_pass = jnp.sum(
        choosers[2][None, None, :, :, None, None, :] * second_pass[:, :, None], axis=3
    )
    return third_pass.reshape((27,) + coarse_shape)


def arrange(blocks, rows, columns):
    pieces = blocks.reshape((rows, columns) + blocks.shape[1:])
    sizes = pieces.shape
    joined = pieces.transpose(2, 3, 0, 4, 1, 5)
    return joined.reshape(sizes[2], sizes[3], rows * sizes[4], columns * sizes[5])


def lower_pad(extended):
    return jnp.pad(extended, ((0, 0), (1, 0), (1, 0), (1, 0)))


def upper_rim_one(level):
    came_z = shifted(level[:, :1], "gz", -1)
    level = jnp.concatenate([level, came_z], axis=1)
    came_y = shifted(level[:, :, :1], "gy", -1)
    level = jnp.concatenate([level, came_y], axis=2)
    came_x = shifted(level[:, :, :, :1], "gx", -1)
    level = jnp.concatenate([level, came_x], axis=3)
    return lower_pad(level)


def shards(coeff_z, coeff_y, coeff_x, reaction):
    count = coeff_z.shape
    rows = lax.axis_size("gy")
    columns = lax.axis_size("gx")
    totals = (count[0] * lax.axis_size("gz"), count[1] * rows, count[2] * columns)
    starts = (
        lax.axis_index("gz") * count[0],
        lax.axis_index("gy") * count[1],
        lax.axis_index("gx") * count[2],
    )
    fine = jnp.stack([coeff_z, coeff_y, coeff_x, reaction])
    rimmed = with_halo(fine, (("gz", 1), ("gy", 2), ("gx", 3)), 1)
    level_one = galerkin(partial(fine_apply, rimmed), starts, count, totals, 9)
    half_count = tuple((value // 2 for value in count))
    half_totals = tuple((value // 2 for value in totals))
    half_starts = tuple((value // 2 for value in starts))
    rimmed_one = upper_rim_one(level_one)
    level_two = galerkin(
        partial(stencil_apply, rimmed_one), half_starts, half_count, half_totals, 9
    )
    quarter_count = tuple((value // 4 for value in count))
    quarter_totals = tuple((value // 4 for value in totals))
    quarter_starts = tuple((value // 4 for value in starts))
    blocks = lax.all_gather(level_two[None], ("gy", "gx"), axis=0, tiled=True)
    slab = arrange(blocks, rows, columns)
    came_slab = shifted(slab[:, :1], "gz", -1)
    extended = jnp.concatenate([slab, came_slab], axis=1)
    padded = jnp.pad(extended, ((0, 0), (1, 0), (1, 1), (1, 1)))
    slab_count = (quarter_count[0], quarter_totals[1], quarter_totals[2])
    level_three = galerkin(
        partial(stencil_apply, padded), (quarter_starts[0], 0, 0), slab_count, quarter_totals, 9
    )
    return (level_one, level_two, level_three)


def solution(mesh):
    in_specs = (P("gz", "gy", "gx"), P("gz", "gy", "gx"), P("gz", "gy", "gx"), P("gz", "gy", "gx"))
    out_specs = (P(None, "gz", "gy", "gx"), P(None, "gz", "gy", "gx"), P(None, "gz", None, None))
    return jax.shard_map(shards, mesh=mesh, in_specs=in_specs, out_specs=out_specs, check_vma=False)
```

profile of v0, /device:TPU:1, one launch (start us, length us, event | category | flops | bytes accessed | tf_op | source)
XLA Modules:
  0.0 670.6 jit_solution(4785951364510372709)
XLA Ops:
  8.1 6.3 collective-permute-start
  50.4 10.4 %pad_maximum_fusion = f32[4,18,34,130]{2,0,3,1:T(4,128)} fusion(f32[4,18,34,1]{2,0,3,1:T(4,128)S(1)} %collective-permute-done.5, f32[4,18,1,128]{2,0,3,1:T(4,128)} %copy.46, f32[4,18,32,128]{2,0,3,1:T(4,128)} %copy.45, f32[4,18,1,128]{2,0,3,1:T(4,128)} %copy.44, f32[4,18,34,1]{2,0,3,1:T(4,128)S(1)} %collective-permute-done.4), kind=kLoop, calls=%fused_computation.342 | loop fusion | flops 1272960 | bytes 2545920 | tf_op jit(solution)/shard_map/concatenate | solution.py:24
  60.9 6.7 copy.47
  67.6 235.2 %while.42 = (s32[]{:T(128)}, f32[3,9,8,16,64]{4,3,2,1,0:T(8,128)}, f32[4,18,34,130]{3,2,1,0:T(8,128)}, s32[3]{0:T(128)S(1)}, pred[129]{0:T(512)(128)(4,1)S(1)}, ...) while((s32[]{:T(128)}, f32[3,9,8,16,64]{4,3,2,1,0:T(8,128)}, ...), condition=%wide.region_4.5_spmd.clone, body=%wide.region_0.4_spmd.clone.sunk | while | flops 16092108 | bytes 49456128 | solution.py:121
  74.9 13.9 %fusion.200 = f32[9,17,33,129]{3,2,1,0:T(8,128)} fusion(f32[9,19,35,131]{3,2,1,0:T(8,128)S(1)} %broadcast_multiply_fusion.13, f32[17,33,129]{2,1,0:T(8,128)} %get-tuple-element.1480, f32[17,33,129]{2,1,0:T(8,128)} %get-tuple-element.1481, f32[17,33,129]{2,1,0:T(8,128)} %get-tuple-element.1482, f32[17,33,129]{2,1,0:T(8,128)} %get-tuple-element.1483, ...), kind=kLoop, calls=%fused_computation.15.clone.1 | loop fusion | flops 13026420 | bytes 22940972 | tf_op jit(solution)/shard_map/while/body/eval_jaxpr/jit(_where)/select_n | solution.py:118
  93.1 6.0 slice.1904
  99.2 6.0 slice.1905
  105.1 5.9 slice.1906
  113.5 10.5 %slice.1907 = f32[9,8,16,64]{3,2,1,0:T(8,128)S(1)} slice(f32[9,8,16,129]{3,2,1,0:T(8,128)S(1)} %multiply_add_fusion.13), slice={[0:9:1], [0:8:1], [0:16:1], [2:129:2]} | slice | bytes 589824 | tf_op jit(solution)/shard_map/while/body/eval_jaxpr/slice | solution.py:53
  124.1 10.5 %slice.1908 = f32[9,8,16,64]{3,2,1,0:T(8,128)S(1)} slice(f32[9,8,16,129]{3,2,1,0:T(8,128)S(1)} %multiply_add_fusion.13), slice={[0:9:1], [0:8:1], [0:16:1], [1:129:2]} | slice | bytes 589824 | tf_op jit(solution)/shard_map/while/body/eval_jaxpr/slice | solution.py:52
  134.6 10.4 %slice.1909 = f32[9,8,16,64]{3,2,1,0:T(8,128)S(1)} slice(f32[9,8,16,129]{3,2,1,0:T(8,128)S(1)} %multiply_add_fusion.13), slice={[0:9:1], [0:8:1], [0:16:1], [0:128:2]} | slice | bytes 589824 | tf_op jit(solution)/shard_map/while/body/eval_jaxpr/slice | solution.py:51
  153.0 13.9 %fusion.200 = f32[9,17,33,129]{3,2,1,0:T(8,128)} fusion(f32[9,19,35,131]{3,2,1,0:T(8,128)S(1)} %broadcast_multiply_fusion.13, f32[17,33,129]{2,1,0:T(8,128)} %get-tuple-element.1480, f32[17,33,129]{2,1,0:T(8,128)} %get-tuple-element.1481, f32[17,33,129]{2,1,0:T(8,128)} %get-tuple-element.1482, f32[17,33,129]{2,1,0:T(8,128)} %get-tuple-element.1483, ...), kind=kLoop, calls=%fused_computation.15.clone.1 | loop fusion | flops 13026420 | bytes 22940972 | tf_op jit(solution)/shard_map/while/body/eval_jaxpr/jit(_where)/select_n | solution.py:118
  171.2 6.0 slice.1904
  177.3 6.0 slice.1905
  183.2 5.9 slice.1906
  191.7 10.5 %slice.1907 = f32[9,8,16,64]{3,2,1,0:T(8,128)S(1)} slice(f32[9,8,16,129]{3,2,1,0:T(8,128)S(1)} %multiply_add_fusion.13), slice={[0:9:1], [0:8:1], [0:16:1], [2:129:2]} | slice | bytes 589824 | tf_op jit(solution)/shard_map/while/body/eval_jaxpr/slice | solution.py:53
  202.2 10.5 %slice.1908 = f32[9,8,16,64]{3,2,1,0:T(8,128)S(1)} slice(f32[9,8,16,129]{3,2,1,0:T(8,128)S(1)} %multiply_add_fusion.13), slice={[0:9:1], [0:8:1], [0:16:1], [1:129:2]} | slice | bytes 589824 | tf_op jit(solution)/shard_map/while/body/eval_jaxpr/slice | solution.py:52
  212.7 10.4 %slice.1909 = f32[9,8,16,64]{3,2,1,0:T(8,128)S(1)} slice(f32[9,8,16,129]{3,2,1,0:T(8,128)S(1)} %multiply_add_fusion.13), slice={[0:9:1], [0:8:1], [0:16:1], [0:128:2]} | slice | bytes 589824 | tf_op jit(solution)/shard_map/while/body/eval_jaxpr/slice | solution.py:51
  231.1 13.9 %fusion.200 = f32[9,17,33,129]{3,2,1,0:T(8,128)} fusion(f32[9,19,35,131]{3,2,1,0:T(8,128)S(1)} %broadcast_multiply_fusion.13, f32[17,33,129]{2,1,0:T(8,128)} %get-tuple-element.1480, f32[17,33,129]{2,1,0:T(8,128)} %get-tuple-element.1481, f32[17,33,129]{2,1,0:T(8,128)} %get-tuple-element.1482, f32[17,33,129]{2,1,0:T(8,128)} %get-tuple-element.1483, ...), kind=kLoop, calls=%fused_computation.15.clone.1 | loop fusion | flops 13026420 | bytes 22940972 | tf_op jit(solution)/shard_map/while/body/eval_jaxpr/jit(_where)/select_n | solution.py:118
  249.4 6.0 slice.1904
  255.4 6.0 slice.1905
  261.4 5.9 slice.1906
  269.8 10.5 %slice.1907 = f32[9,8,16,64]{3,2,1,0:T(8,128)S(1)} slice(f32[9,8,16,129]{3,2,1,0:T(8,128)S(1)} %multiply_add_fusion.13), slice={[0:9:1], [0:8:1], [0:16:1], [2:129:2]} | slice | bytes 589824 | tf_op jit(solution)/shard_map/while/body/eval_jaxpr/slice | solution.py:53
  280.3 10.5 %slice.1908 = f32[9,8,16,64]{3,2,1,0:T(8,128)S(1)} slice(f32[9,8,16,129]{3,2,1,0:T(8,128)S(1)} %multiply_add_fusion.13), slice={[0:9:1], [0:8:1], [0:16:1], [1:129:2]} | slice | bytes 589824 | tf_op jit(solution)/shard_map/while/body/eval_jaxpr/slice | solution.py:52
  290.9 10.4 %slice.1909 = f32[9,8,16,64]{3,2,1,0:T(8,128)S(1)} slice(f32[9,8,16,129]{3,2,1,0:T(8,128)S(1)} %multiply_add_fusion.13), slice={[0:9:1], [0:8:1], [0:16:1], [0:128:2]} | slice | bytes 589824 | tf_op jit(solution)/shard_map/while/body/eval_jaxpr/slice | solution.py:51
  308.2 9.3 %collective-permute-done.6 = f32[27,1,16,64]{3,2,1,0:T(8,128)S(1)} collective-permute-done((f32[27,1,16,64]{3,2,1,0:T(8,128)S(1)}, f32[27,1,16,64]{3,2,1,0:T(8,128)S(1)}, u32[]{:S(2)}, u32[]{:S(2)}) %collective-permute-start.6) | collective-permute-done | bytes 110624 | tf_op jit(solution)/shard_map/ppermute | solution.py:12
  335.0 5.5 select_maximum_fusion.1
  340.5 122.8 %while.43 = (s32[]{:T(128)}, f32[3,9,4,8,32]{4,3,2,1,0:T(8,128)}, f32[27,10,18,66]{3,2,1,0:T(8,128)S(1)}, s32[3]{0:T(128)S(1)}, pred[65]{0:T(512)(128)(4,1)S(1)}...) while((s32[]{:T(128)}, f32[3,9,4,8,32]{4,3,2,1,0:T(8,128)}, ...), condition=%wide.region_12.13_spmd.clone, body=%wide.region_8.12_spmd.clone.sunk | while | flops 5258814 | bytes 15993919 | solution.py:121
  345.9 5.0 fusion.204
  351.8 5.0 slice.1942
  361.7 4.9 slice.1944
  386.8 5.0 fusion.204
  392.7 5.0 slice.1942
  402.6 4.9 slice.1944
  427.7 5.0 fusion.204
  433.6 5.0 slice.1942
  466.1 56.5 %all-gather.2.cloned.1.call-done = f32[16,27,4,8,32]{4,3,2,1,0:T(8,128)} async-done(((f32[1,27,4,8,32]{4,3,2,1,0:T(8,128)}), f32[16,27,4,8,32]{4,3,2,1,0:T(8,128)}) %all-gather.2.cloned.1.call-update) | async-done | bytes 1769488 | tf_op jit(solution)/shard_map/all_gather | solution.py:185
  522.7 11.7 %copy.52 = f32[27,4,4,8,4,32]{5,4,3,2,1,0:T(4,128)} copy(f32[27,4,4,8,4,32]{5,3,1,0,4,2:T(8,128)} %bitcast.172) | data formatting | bytes 3538944 | tf_op jit(solution)/shard_map/transpose | solution.py:144
  534.3 5.6 reshape.1454
  541.3 13.6 %collective-permute-done.9 = f32[27,1,32,128]{3,2,1,0:T(8,128)S(1)} collective-permute-done((f32[27,1,32,128]{3,2,1,0:T(8,128)S(1)}, f32[27,1,32,128]{3,2,1,0:T(8,128)S(1)}, u32[]{:S(2)}, u32[]{:S(2)}) %collective-permute-start.9) | collective-permute-done | bytes 442400 | tf_op jit(solution)/shard_map/ppermute | solution.py:12
  555.0 5.9 select_maximum_fusion
  560.8 100.3 %while.44 = (s32[]{:T(128)}, f32[3,9,2,16,64]{4,3,2,1,0:T(8,128)}, f32[27,6,34,130]{3,2,1,0:T(8,128)}, s32[3]{0:T(128)S(1)}, pred[129]{0:T(512)(128)(4,1)S(1)}, ...) while((s32[]{:T(128)}, f32[3,9,2,16,64]{4,3,2,1,0:T(8,128)}, ...), condition=%wide.region_20.21_spmd.clone, body=%wide.region_16.20_spmd.clone.sunk | while | flops 11217438 | bytes 33119696 | solution.py:121
  563.5 5.1 slice_bitcast_fusion.69
  571.8 10.8 %fusion.208 = f32[9,5,33,129]{3,2,1,0:T(8,128)S(1)} fusion(f32[9,7,35,131]{3,2,1,0:T(8,128)S(1)} %broadcast_multiply_fusion.17, f32[5,33,129]{2,1,0:T(8,128)} %get-tuple-element.1566, f32[5,33,129]{2,1,0:T(8,128)} %get-tuple-element.1567, f32[5,33,129]{2,1,0:T(8,128)} %get-tuple-element.1568, f32[5,33,129]{2,1,0:T(8,128)} %get-tuple-element.1569, ...), kind=kLoop, calls=%fused_computation.207.clone.1 | loop fusion | flops 10344510 | bytes 23775344 | tf_op jit(solution)/shard_map/while/body/eval_jaxpr/jit(_where)/select_n | solution.py:118
  596.9 5.1 slice_bitcast_fusion.69
  605.2 10.8 %fusion.208 = f32[9,5,33,129]{3,2,1,0:T(8,128)S(1)} fusion(f32[9,7,35,131]{3,2,1,0:T(8,128)S(1)} %broadcast_multiply_fusion.17, f32[5,33,129]{2,1,0:T(8,128)} %get-tuple-element.1566, f32[5,33,129]{2,1,0:T(8,128)} %get-tuple-element.1567, f32[5,33,129]{2,1,0:T(8,128)} %get-tuple-element.1568, f32[5,33,129]{2,1,0:T(8,128)} %get-tuple-element.1569, ...), kind=kLoop, calls=%fused_computation.207.clone.1 | loop fusion | flops 10344510 | bytes 23775344 | tf_op jit(solution)/shard_map/while/body/eval_jaxpr/jit(_where)/select_n | solution.py:118
  630.3 5.1 slice_bitcast_fusion.69
  638.7 10.8 %fusion.208 = f32[9,5,33,129]{3,2,1,0:T(8,128)S(1)} fusion(f32[9,7,35,131]{3,2,1,0:T(8,128)S(1)} %broadcast_multiply_fusion.17, f32[5,33,129]{2,1,0:T(8,128)} %get-tuple-element.1566, f32[5,33,129]{2,1,0:T(8,128)} %get-tuple-element.1567, f32[5,33,129]{2,1,0:T(8,128)} %get-tuple-element.1568, f32[5,33,129]{2,1,0:T(8,128)} %get-tuple-element.1569, ...), kind=kLoop, calls=%fused_computation.207.clone.1 | loop fusion | flops 10344510 | bytes 23775344 | tf_op jit(solution)/shard_map/while/body/eval_jaxpr/jit(_where)/select_n | solution.py:118
  (531 shorter events, 237.5 us)
Async XLA Ops:
  7.2 515.5 %all-gather.2.cloned.1.call-start = ((), (), s32[]{:S(2)}) async-start(), calls=%async_computation | async-start | bytes 7520256 | tf_op jit(solution)/shard_map/all_gather | solution.py:185
  8.1 15.9 %collective-permute-start = (f32[4,1,32,128]{3,2,1,0:T(8,128)S(1)}, f32[4,1,32,128]{3,2,1,0:T(8,128)S(1)}, u32[]{:S(2)}, u32[]{:S(2)}) collective-permute-start(f32[4,1,32,128]{3,2,1,0:T(8,128)S(1)} %get-tuple-element.968), channel_id=1, source_target_pairs={{0,16},{16,32},{32,48},{48,64},{64,80},{80,96},{96,112},{1,17},{17... | collective-permute-start | bytes 196616 | tf_op jit(solution)/shard_map/ppermute | solution.py:20
  14.4 9.6 %collective-permute-start.1 = (f32[4,1,32,128]{3,2,1,0:T(8,128)S(1)}, f32[4,1,32,128]{3,2,1,0:T(8,128)S(1)}, u32[]{:S(2)}, u32[]{:S(2)}) collective-permute-start(f32[4,1,32,128]{3,2,1,0:T(8,128)S(1)} %get-tuple-element.969), channel_id=1, source_target_pairs={{16,0},{32,16},{48,32},{64,48},{80,64},{96,80},{112,96},{17,1},{33... | collective-permute-start | bytes 196616 | tf_op jit(solution)/shard_map/ppermute | solution.py:23
  25.4 9.4 %collective-permute-start.2 = (f32[4,18,1,128]{3,0,2,1:T(4,128)S(1)}, f32[4,18,1,128]{3,0,2,1:T(4,128)S(1)}, u32[]{:S(2)}, u32[]{:S(2)}) collective-permute-start(f32[4,18,1,128]{3,0,2,1:T(4,128)S(1)} %copy.53), channel_id=1, source_target_pairs={{0,4},{4,8},{8,12},{1,5},{5,9},{9,13},{2,6},{6,10},{10,14},{3,7},{... | collective-permute-start | bytes 110600 | tf_op jit(solution)/shard_map/ppermute | solution.py:20
  28.9 9.2 %collective-permute-start.3 = (f32[4,18,1,128]{3,0,2,1:T(4,128)S(1)}, f32[4,18,1,128]{3,0,2,1:T(4,128)S(1)}, u32[]{:S(2)}, u32[]{:S(2)}) collective-permute-start(f32[4,18,1,128]{3,0,2,1:T(4,128)S(1)} %copy.54), channel_id=1, source_target_pairs={{4,0},{8,4},{12,8},{5,1},{9,5},{13,9},{6,2},{10,6},{14,10},{7,3},{... | collective-permute-start | bytes 110600 | tf_op jit(solution)/shard_map/ppermute | solution.py:23
  42.5 4.5 collective-permute-start.4
  45.7 4.7 collective-permute-start.5
  67.6 235.2 %copy-start.7 = (f32[3,3,8]{2,1,0:T(4,128)S(1)}, f32[3,3,8]{2,1,0:T(4,128)}, u32[]{:S(2)}) copy-start(f32[3,3,8]{2,1,0:T(4,128)} %fusion.139) | copy-start | bytes 868
  306.3 18.1 %copy-start.1 = (f32[3,3,3,8,16,64]{5,4,3,2,1,0:T(8,128)}, f32[3,3,3,8,16,64]{5,4,3,2,1,0:T(8,128)S(1)}, u32[]{:S(2)}) copy-start(f32[3,3,3,8,16,64]{5,4,3,2,1,0:T(8,128)S(1)} %multiply_reduce_fusion) | copy-start | bytes 2654212
  306.3 11.2 %collective-permute-start.6 = (f32[27,1,16,64]{3,2,1,0:T(8,128)S(1)}, f32[27,1,16,64]{3,2,1,0:T(8,128)S(1)}, u32[]{:S(2)}, u32[]{:S(2)}) collective-permute-start(f32[27,1,16,64]{3,2,1,0:T(8,128)S(1)} %slice.1417), channel_id=1, source_target_pairs={{16,0},{32,16},{48,32},{64,48},{80,64},{96,80},{112,96},{17,1},{33... | collective-permute-start | bytes 331784 | tf_op jit(solution)/shard_map/ppermute | solution.py:12
  317.7 6.7 collective-permute-start.7
  326.5 5.5 collective-permute-start.8
  340.5 122.9 %copy-start.4 = (f32[3,3,4]{2,1,0:T(4,128)S(1)}, f32[3,3,4]{2,1,0:T(4,128)}, u32[]{:S(2)}) copy-start(f32[3,3,4]{2,1,0:T(4,128)} %fusion.142) | copy-start | bytes 436
  340.5 124.1 %copy-start.5 = (f32[3,3,8]{2,1,0:T(4,128)S(1)}, f32[3,3,8]{2,1,0:T(4,128)}, u32[]{:S(2)}) copy-start(f32[3,3,8]{2,1,0:T(4,128)} %fusion.141) | copy-start | bytes 868
  340.5 124.3 %copy-start.6 = (f32[3,3,32]{2,1,0:T(4,128)S(1)}, f32[3,3,32]{2,1,0:T(4,128)}, u32[]{:S(2)}) copy-start(f32[3,3,32]{2,1,0:T(4,128)} %fusion.140) | copy-start | bytes 3460
  540.0 15.0 %collective-permute-start.9 = (f32[27,1,32,128]{3,2,1,0:T(8,128)S(1)}, f32[27,1,32,128]{3,2,1,0:T(8,128)S(1)}, u32[]{:S(2)}, u32[]{:S(2)}) collective-permute-start(f32[27,1,32,128]{3,2,1,0:T(8,128)S(1)} %slice.1418), channel_id=1, source_target_pairs={{16,0},{32,16},{48,32},{64,48},{80,64},{96,80},{112,96},{17,1},{33... | collective-permute-start | bytes 1327112 | tf_op jit(solution)/shard_map/ppermute | solution.py:12
  583.1 11.0 %copy-start.13 = (pred[7]{0:T(512)(128)(4,1)S(1)}, pred[7]{0:T(512)(128)(4,1)}, u32[]{:S(2)}) copy-start(pred[7]{0:T(512)(128)(4,1)} %copy-done.12) | copy-start | bytes 25 | tf_op jit(solution)/shard_map/while
  583.1 11.0 %copy-start.15 = (pred[7]{0:T(512)(128)(4,1)S(1)}, pred[7]{0:T(512)(128)(4,1)}, u32[]{:S(2)}) copy-start(pred[7]{0:T(512)(128)(4,1)} %copy-done.14) | copy-start | bytes 25 | tf_op jit(solution)/shard_map/while
  583.1 11.0 %copy-start.17 = (pred[7]{0:T(512)(128)(4,1)S(1)}, pred[7]{0:T(512)(128)(4,1)}, u32[]{:S(2)}) copy-start(pred[7]{0:T(512)(128)(4,1)} %copy-done.16) | copy-start | bytes 25 | tf_op jit(solution)/shard_map/while
  583.1 11.0 %copy-start.19 = (pred[7]{0:T(512)(128)(4,1)S(1)}, pred[7]{0:T(512)(128)(4,1)}, u32[]{:S(2)}) copy-start(pred[7]{0:T(512)(128)(4,1)} %copy-done.18) | copy-start | bytes 25 | tf_op jit(solution)/shard_map/while
  583.1 11.0 %copy-start.21 = (s32[35]{0:T(128)S(1)}, s32[35]{0:T(128)}, u32[]{:S(2)}) copy-start(s32[35]{0:T(128)} %copy-done.20) | copy-start | bytes 424 | tf_op jit(solution)/shard_map/while
  583.1 11.0 %copy-start.23 = (s32[35]{0:T(128)S(1)}, s32[35]{0:T(128)}, u32[]{:S(2)}) copy-start(s32[35]{0:T(128)} %copy-done.22) | copy-start | bytes 424 | tf_op jit(solution)/shard_map/while
  583.1 11.0 %copy-start.25 = (pred[35]{0:T(512)(128)(4,1)S(1)}, pred[35]{0:T(512)(128)(4,1)}, u32[]{:S(2)}) copy-start(pred[35]{0:T(512)(128)(4,1)} %copy-done.24) | copy-start | bytes 109 | tf_op jit(solution)/shard_map/while
  583.2 11.0 %copy-start.27 = (pred[35]{0:T(512)(128)(4,1)S(1)}, pred[35]{0:T(512)(128)(4,1)}, u32[]{:S(2)}) copy-start(pred[35]{0:T(512)(128)(4,1)} %copy-done.26) | copy-start | bytes 109 | tf_op jit(solution)/shard_map/while
  583.2 11.0 %copy-start.29 = (pred[35]{0:T(512)(128)(4,1)S(1)}, pred[35]{0:T(512)(128)(4,1)}, u32[]{:S(2)}) copy-start(pred[35]{0:T(512)(128)(4,1)} %copy-done.28) | copy-start | bytes 109 | tf_op jit(solution)/shard_map/while
  583.2 11.0 %copy-start.31 = (pred[35]{0:T(512)(128)(4,1)S(1)}, pred[35]{0:T(512)(128)(4,1)}, u32[]{:S(2)}) copy-start(pred[35]{0:T(512)(128)(4,1)} %copy-done.30) | copy-start | bytes 109 | tf_op jit(solution)/shard_map/while
  583.2 11.0 %copy-start.33 = (pred[131]{0:T(512)(128)(4,1)S(1)}, pred[131]{0:T(512)(128)(4,1)}, u32[]{:S(2)}) copy-start(pred[131]{0:T(512)(128)(4,1)} %copy-done.32) | copy-start | bytes 397 | tf_op jit(solution)/shard_map/while
  583.2 11.0 %copy-start.35 = (pred[131]{0:T(512)(128)(4,1)S(1)}, pred[131]{0:T(512)(128)(4,1)}, u32[]{:S(2)}) copy-start(pred[131]{0:T(512)(128)(4,1)} %copy-done.34) | copy-start | bytes 397 | tf_op jit(solution)/shard_map/while
  583.2 11.0 %copy-start.37 = (pred[131]{0:T(512)(128)(4,1)S(1)}, pred[131]{0:T(512)(128)(4,1)}, u32[]{:S(2)}) copy-start(pred[131]{0:T(512)(128)(4,1)} %copy-done.36) | copy-start | bytes 397 | tf_op jit(solution)/shard_map/while
  583.2 11.0 %copy-start.39 = (pred[131]{0:T(512)(128)(4,1)S(1)}, pred[131]{0:T(512)(128)(4,1)}, u32[]{:S(2)}) copy-start(pred[131]{0:T(512)(128)(4,1)} %copy-done.38) | copy-start | bytes 397 | tf_op jit(solution)/shard_map/while
  583.2 11.0 %copy-start.41 = (s32[3]{0:T(128)S(1)}, s32[3]{0:T(128)}, u32[]{:S(2)}) copy-start(s32[3]{0:T(128)} %copy-done.40) | copy-start | bytes 40 | tf_op jit(solution)/shard_map/while
  616.5 11.0 %copy-start.13 = (pred[7]{0:T(512)(128)(4,1)S(1)}, pred[7]{0:T(512)(128)(4,1)}, u32[]{:S(2)}) copy-start(pred[7]{0:T(512)(128)(4,1)} %copy-done.12) | copy-start | bytes 25 | tf_op jit(solution)/shard_map/while
  616.5 11.0 %copy-start.15 = (pred[7]{0:T(512)(128)(4,1)S(1)}, pred[7]{0:T(512)(128)(4,1)}, u32[]{:S(2)}) copy-start(pred[7]{0:T(512)(128)(4,1)} %copy-done.14) | copy-start | bytes 25 | tf_op jit(solution)/shard_map/while
  616.5 11.0 %copy-start.17 = (pred[7]{0:T(512)(128)(4,1)S(1)}, pred[7]{0:T(512)(128)(4,1)}, u32[]{:S(2)}) copy-start(pred[7]{0:T(512)(128)(4,1)} %copy-done.16) | copy-start | bytes 25 | tf_op jit(solution)/shard_map/while
  616.6 11.0 %copy-start.19 = (pred[7]{0:T(512)(128)(4,1)S(1)}, pred[7]{0:T(512)(128)(4,1)}, u32[]{:S(2)}) copy-start(pred[7]{0:T(512)(128)(4,1)} %copy-done.18) | copy-start | bytes 25 | tf_op jit(solution)/shard_map/while
  616.6 11.0 %copy-start.21 = (s32[35]{0:T(128)S(1)}, s32[35]{0:T(128)}, u32[]{:S(2)}) copy-start(s32[35]{0:T(128)} %copy-done.20) | copy-start | bytes 424 | tf_op jit(solution)/shard_map/while
  616.6 11.0 %copy-start.23 = (s32[35]{0:T(128)S(1)}, s32[35]{0:T(128)}, u32[]{:S(2)}) copy-start(s32[35]{0:T(128)} %copy-done.22) | copy-start | bytes 424 | tf_op jit(solution)/shard_map/while
  616.6 11.0 %copy-start.25 = (pred[35]{0:T(512)(128)(4,1)S(1)}, pred[35]{0:T(512)(128)(4,1)}, u32[]{:S(2)}) copy-start(pred[35]{0:T(512)(128)(4,1)} %copy-done.24) | copy-start | bytes 109 | tf_op jit(solution)/shard_map/while
  616.6 11.0 %copy-start.27 = (pred[35]{0:T(512)(128)(4,1)S(1)}, pred[35]{0:T(512)(128)(4,1)}, u32[]{:S(2)}) copy-start(pred[35]{0:T(512)(128)(4,1)} %copy-done.26) | copy-start | bytes 109 | tf_op jit(solution)/shard_map/while
  616.6 11.0 %copy-start.29 = (pred[35]{0:T(512)(128)(4,1)S(1)}, pred[35]{0:T(512)(128)(4,1)}, u32[]{:S(2)}) copy-start(pred[35]{0:T(512)(128)(4,1)} %copy-done.28) | copy-start | bytes 109 | tf_op jit(solution)/shard_map/while
  616.6 11.0 %copy-start.31 = (pred[35]{0:T(512)(128)(4,1)S(1)}, pred[35]{0:T(512)(128)(4,1)}, u32[]{:S(2)}) copy-start(pred[35]{0:T(512)(128)(4,1)} %copy-done.30) | copy-start | bytes 109 | tf_op jit(solution)/shard_map/while
  616.6 11.0 %copy-start.33 = (pred[131]{0:T(512)(128)(4,1)S(1)}, pred[131]{0:T(512)(128)(4,1)}, u32[]{:S(2)}) copy-start(pred[131]{0:T(512)(128)(4,1)} %copy-done.32) | copy-start | bytes 397 | tf_op jit(solution)/shard_map/while
  616.6 11.0 %copy-start.35 = (pred[131]{0:T(512)(128)(4,1)S(1)}, pred[131]{0:T(512)(128)(4,1)}, u32[]{:S(2)}) copy-start(pred[131]{0:T(512)(128)(4,1)} %copy-done.34) | copy-start | bytes 397 | tf_op jit(solution)/shard_map/while
  616.6 11.0 %copy-start.37 = (pred[131]{0:T(512)(128)(4,1)S(1)}, pred[131]{0:T(512)(128)(4,1)}, u32[]{:S(2)}) copy-start(pred[131]{0:T(512)(128)(4,1)} %copy-done.36) | copy-start | bytes 397 | tf_op jit(solution)/shard_map/while
  650.0 11.0 %copy-start.13 = (pred[7]{0:T(512)(128)(4,1)S(1)}, pred[7]{0:T(512)(128)(4,1)}, u32[]{:S(2)}) copy-start(pred[7]{0:T(512)(128)(4,1)} %copy-done.12) | copy-start | bytes 25 | tf_op jit(solution)/shard_map/while
  650.0 11.0 %copy-start.15 = (pred[7]{0:T(512)(128)(4,1)S(1)}, pred[7]{0:T(512)(128)(4,1)}, u32[]{:S(2)}) copy-start(pred[7]{0:T(512)(128)(4,1)} %copy-done.14) | copy-start | bytes 25 | tf_op jit(solution)/shard_map/while
  650.0 11.0 %copy-start.17 = (pred[7]{0:T(512)(128)(4,1)S(1)}, pred[7]{0:T(512)(128)(4,1)}, u32[]{:S(2)}) copy-start(pred[7]{0:T(512)(128)(4,1)} %copy-done.16) | copy-start | bytes 25 | tf_op jit(solution)/shard_map/while
  650.0 11.0 %copy-start.19 = (pred[7]{0:T(512)(128)(4,1)S(1)}, pred[7]{0:T(512)(128)(4,1)}, u32[]{:S(2)}) copy-start(pred[7]{0:T(512)(128)(4,1)} %copy-done.18) | copy-start | bytes 25 | tf_op jit(solution)/shard_map/while
  (67 other events, 500.4 us)
Sparse Core Ops, SparseCore 0:
  465.9 56.7 all-gather.1
where the time goes:
time: 680 us; the launch traced here: 671 us
  local copies, waits for them, and re-layouts  344 us (51%)
  other arithmetic  188 us (28%)
  waiting for transfers between devices  91.2 us (13%)
  starting transfers between devices  23.4 us (3%)
  between operations  15 us (2%)
  loops' own time  9.05 us (1%)
    select_n x9, other arithmetic, colour_block(): image = jnp.where(inside[None], apply_fn(field, count), 0.0)  89.3 us
    slice x18, local copies, waits for them, and re-layouts, restrict_axis(): upper = lax.slice_in_dim(field, 2, length + 1, 2, axis)  87.4 us
    slice x18, local copies, waits for them, and re-layouts, restrict_axis(): middle = lax.slice_in_dim(field, 1, length + 1, 2, axis)  86.4 us
    slice x18, local copies, waits for them, and re-layouts, restrict_axis(): lower = lax.slice_in_dim(field, 0, length, 2, axis)  85.8 us
    all_gather x1, waiting for transfers between devices, shards(): blocks = lax.all_gather(level_two[None], ('gy', 'gx'), axis=0, tiled=True)  56.5 us
    ppermute x4, waiting for transfers between devices, shifted(): return lax.ppermute(block, axis, route)  31.2 us
    mul x12, local copies, waits for them, and re-layouts, stencil_apply(): window(padded[offset:offset + 1], (1, 1, 1), count)  27 us
    add x18, other arithmetic, restrict_axis(): return 0.5 * lower + middle + 0.5 * upper  26.7 us
  transfers between devices with their start and end apart: 11, of which 6 were waited for; matrix products, arithmetic and copies ran while one was open for 3% of the time, Pallas kernels for 0%

commit v1 on v0

v1 whole, which is shorter than its diff:
```python
from functools import partial

import jax
import jax.numpy as jnp
import ml_dtypes
import numpy as np
from jax import lax
from jax.experimental import pallas as pl
from jax.experimental.pallas import tpu as pltpu
from jax.sharding import PartitionSpec as P

MESH = pl.DeviceIdType.MESH
F32 = jnp.float32
BF16 = jnp.bfloat16


def forms(level, n):
    step = 1 << level
    i = np.arange(n)

    def hat(i, index):
        return np.maximum(0.0, 1.0 - np.abs(i - (step * index + step - 1)) / step)

    def slope(i, index):
        return hat(i, index) - hat(i + 1, index)

    def column(plus, index):
        other = index + plus
        return hat(i, index) * hat(i, other), slope(i, index) * slope(i, other)

    return column


def row_order(count):
    return (
        [(0, j) for j in range(count)]
        + [(1, j) for j in range(-1, count)]
        + [(0, -1), (0, count)]
    )


def weights_y(level, n, rows):
    column = forms(level, n)
    mass = np.zeros((rows, n))
    stiff = np.zeros((rows, n))
    for row, (plus, index) in enumerate(row_order(n >> level)):
        mass[row], stiff[row] = column(plus, index)
    first = np.concatenate([mass, mass, stiff, stiff], axis=1)
    second = np.concatenate([mass, mass], axis=1)
    return first.astype(ml_dtypes.bfloat16), second.astype(ml_dtypes.bfloat16)


def lanes_of(level, n):
    count = n >> level
    if level == 3:
        return [(0, j) for j in range(-1, count + 1)] + [(1, j) for j in range(-1, count)], 128
    rim = 2 * count
    lanes = [(0, j) for j in range(count)] + [(1, j) for j in range(count)]
    lanes += [None] * (2 * count)
    lanes[rim] = (0, -1)
    lanes[rim + count // 2] = (0, count)
    lanes[rim + count] = (1, -1)
    return lanes, 4 * count


def weights_x(level, n):
    column = forms(level, n)
    lanes, width = lanes_of(level, n)
    mass = np.zeros((n, width))
    stiff = np.zeros((n, width))
    for lane, entry in enumerate(lanes):
        if entry is not None:
            mass[:, lane], stiff[:, lane] = column(*entry)
    scale = 0.5**level
    both = np.concatenate([mass, mass, stiff, stiff], axis=0) * scale
    return both.astype(ml_dtypes.bfloat16)


def place_x(blocks, count):
    whole = blocks * count
    out = np.zeros((blocks, 2, 128, 3 * 128))
    for block in range(blocks):
        for layer in range(3):
            entries = lanes_of(3, count * 8)[0]
            for lane, (plus, index) in enumerate(entries):
                source = 40 * layer + lane
                target = block * count + index
                if 0 <= target < whole:
                    out[block, :, source, layer * 128 + plus * whole + target] = 1.0
                if plus == 0 and target == whole:
                    out[block, :, source, layer * 128 + whole - 1] = 63.0
                    out[block, :, source, layer * 128 + 2 * whole - 1] = 1.0
    return out.reshape(blocks * 256, 384).astype(ml_dtypes.bfloat16)


def place_y(blocks, count, rows, packed):
    whole = blocks * count
    out = np.zeros((rows, 2, blocks, packed))
    for block in range(blocks):
        for row, (plus, index) in enumerate(row_order(count)):
            target = block * count + index
            if 0 <= target < whole:
                out[target + plus * (whole + 1), :, block, row] = 1.0
            if plus == 0 and target == whole:
                out[whole - 1, :, block, row] = 63.0
                out[2 * whole, :, block, row] = 1.0
    return out.reshape(rows, 2 * blocks * packed).astype(ml_dtypes.bfloat16)


def split(value):
    high = value.astype(BF16)
    return high, (value - high.astype(F32)).astype(BF16)


def dot(left, right):
    return jnp.dot(left, right, preferred_element_type=F32)


def roll(value, shift):
    return pltpu.roll(value, shift % 128, 1)


def mass_layers(field):
    n = len(field)
    quarter = [0.25 * field[2 * j] for j in range(n // 2)] + [None]
    same = {-1: quarter[0]}
    plus = {-1: quarter[0]}
    for j in range(n // 2):
        total = field[2 * j + 1] + quarter[j]
        same[j] = total if quarter[j + 1] is None else total + quarter[j + 1]
        plus[j] = quarter[j + 1]
    same[n // 2] = None
    return same, plus


def stiff_layers(field):
    n = len(field)
    share = {-1: 0.25 * field[0], n // 2 - 1: 0.25 * field[n - 1]}
    for j in range(n // 2 - 1):
        share[j] = 0.25 * (field[2 * j + 1] + field[2 * j + 2])
    same = {-1: share[-1], n // 2: share[n // 2 - 1]}
    for j in range(n // 2):
        same[j] = share[j - 1] + share[j]
    return same, share


def plus_of(a, b):
    if a is None:
        return b
    return a if b is None else a + b


def coarser(same, plus, count):
    def scaled(value, factor):
        return None if value is None else factor * value

    new_same, new_plus = {}, {}
    half = count // 2
    for j in range(-1, half + 1):
        total = scaled(plus_of(same.get(2 * j), same.get(2 * j + 2)), 0.25)
        for term in (same.get(2 * j + 1), plus.get(2 * j), plus.get(2 * j + 1)):
            total = plus_of(total, term)
        new_same[j] = total
    for j in range(-1, half):
        total = scaled(plus_of(plus.get(2 * j + 1), plus.get(2 * j + 2)), 0.5)
        new_plus[j] = plus_of(total, scaled(same.get(2 * j + 2), 0.25))
    return new_same, new_plus


def main_kernel(
    r_ref, kz_ref, ky_ref, kx_ref,
    wy1a, wy1b, wy2a, wy2b, wy3a, wy3b, wx1, wx2, wx3,
    t1, x1, t2, x2, g3,
    ga1, gb1, ga2, gb2, ga3, gb3, c1, c2, c3,
    zu, zl, zr2, zr3, y1, y1r, y2, y2r, px1, px1r, px2, px2r, p3,
    send, recv, gsend, grecv,
):
    gz, gy, gx = lax.axis_index("gz"), lax.axis_index("gy"), lax.axis_index("gx")
    nz, ny, nx = lax.axis_size("gz"), lax.axis_size("gy"), lax.axis_size("gx")
    up_z, down_z = (lax.rem(gz + 1, nz), gy, gx), (lax.rem(gz + nz - 1, nz), gy, gx)
    up_y, down_y = (gz, lax.rem(gy + 1, ny), gx), (gz, lax.rem(gy + ny - 1, ny), gx)
    up_x, down_x = (gz, gy, lax.rem(gx + 1, nx)), (gz, gy, lax.rem(gx + nx - 1, nx))
    slab = ny * nx
    me = gy * nx + gx
    peers = []
    for d in range(1, slab):
        t = lax.rem(me + d, slab)
        peers.append((gz, lax.div(t, nx), lax.rem(t, nx)))

    barrier = pltpu.get_barrier_semaphore()
    for device in peers + [up_z, down_z]:
        pl.semaphore_signal(barrier, inc=1, device_id=device, device_id_type=MESH)
    pl.semaphore_wait(barrier, slab + 1)

    started = []

    def copy(src, dst, device):
        k = len(started)
        c = pltpu.make_async_remote_copy(
            src_ref=src, dst_ref=dst, send_sem=send.at[k], recv_sem=recv.at[k],
            device_id=device, device_id_type=MESH,
        )
        c.start()
        started.append(c)
        return c

    raw = [
        copy(f.at[0], zu.at[j], down_z) for j, f in enumerate((r_ref, kz_ref, ky_ref, kx_ref))
    ]
    raw.append(copy(kz_ref.at[15], zl, up_z))

    def layers(ref):
        return [ref[j] for j in range(16)]

    kz_layers = layers(kz_ref)
    same1, plus1 = mass_layers(layers(r_ref))
    ssame, share = stiff_layers(kz_layers)
    for j in range(-1, 9):
        same1[j] = plus_of(same1[j], ssame[j])
    for j in range(-1, 8):
        plus1[j] = -share[j] if plus1[j] is None else plus1[j] - share[j]
    level1 = [(same1, plus1), mass_layers(layers(ky_ref)), mass_layers(layers(kx_ref))]
    level2 = [coarser(*f, 8) for f in level1]
    level3 = [coarser(*f, 4) for f in level2]

    zero = jnp.zeros((32, 128), F32)

    def put(ga, gb, j, fields):
        lanes = pl.ds(128 * j, 128)
        for base, (ref, value) in enumerate(zip((ga, ga, gb), fields)):
            high, low = split(zero if value is None else value)
            start = 64 * base if base < 2 else 0
            ref[start:start + 32, lanes] = high
            ref[start + 32:start + 64, lanes] = low

    def reduce_yx(ga, gb, wya, wyb, wx, count, rows):
        first = dot(wya[...], ga[...])
        second = dot(wyb[...], gb[...])
        left = []
        for value in (first, second):
            stacked = jnp.concatenate(
                [value[:, 128 * j:128 * j + 128] for j in range(count)], axis=0
            )
            left += split(stacked)
        out = dot(jnp.concatenate(left, axis=1), wx[...])
        return out.reshape(count, rows, out.shape[1])

    for j, (plus, index) in enumerate(row_order(2)):
        put(ga3, gb3, j, [f[plus][index] for f in level3])
    c3[...] = reduce_yx(ga3, gb3, wy3a, wy3b, wx3, 7, 16)
    for j, (plus, index) in enumerate(row_order(4)):
        put(ga2, gb2, j, [f[plus][index] for f in level2])
    c2[...] = reduce_yx(ga2, gb2, wy2a, wy2b, wx2, 11, 32)

    round_z = [
        copy(c2.at[9, 0:24], zr2.at[0], down_z),
        copy(c2.at[4, 0:24], zr2.at[1], down_z),
        copy(c2.at[10, 0:24], zr2.at[2], up_z),
        copy(c3.at[5], zr3.at[0], down_z),
        copy(c3.at[2], zr3.at[1], down_z),
        copy(c3.at[6], zr3.at[2], up_z),
    ]

    top_z, low_z = gz == nz - 1, gz == 0
    for c in raw:
        c.wait_recv()
    last = share[7]
    up_r, up_kz = 0.25 * zu[0], 0.25 * zu[1]
    up_ky, up_kx = 0.25 * zu[2], 0.25 * zu[3]
    come = jnp.where(low_z, 0.0, 0.25 * zl[...])
    add_same = [jnp.where(top_z, 3.0 * last, up_r + up_kz)]
    add_plus = [jnp.where(top_z, last, up_r - up_kz)]
    for f in (up_ky, up_kx):
        add_same.append(jnp.where(top_z, 0.0, f))
        add_plus.append(add_same[-1])
    for f in range(3):
        same, plus = level1[f]
        same[7] = plus_of(same[7], add_same[f])
        plus[7] = plus_of(plus[7], add_plus[f])
        if f == 0:
            same[0] = same[0] + come
            plus[-1] = plus[-1] - come
        plus[-1] = jnp.where(low_z, 0.0, plus[-1])

    for j, (plus, index) in enumerate(row_order(8)[:17]):
        put(ga1, gb1, j, [f[plus][index] for f in level1])
    c1[...] = reduce_yx(ga1, gb1, wy1a, wy1b, wx1, 17, 48)

    for c in round_z:
        c.wait_recv()

    def fix_z(c, came, n, rows, factor):
        same_up, plus_up, share_low = came[0], came[1], came[2]
        rim = c[2 * n + 2, 0:rows]
        low = jnp.where(low_z, 0.0, share_low)
        out = {
            n - 1: c[n - 1, 0:rows] + jnp.where(top_z, factor * rim, same_up),
            2 * n: c[2 * n, 0:rows] + jnp.where(top_z, rim, plus_up),
            n: jnp.where(low_z, 0.0, c[n, 0:rows] - low),
        }
        for k, value in out.items():
            pass
        return out, low

    for c in round_z:
        c.wait_send()
    out2, low2 = fix_z(c2, zr2, 4, 24, 15.0)
    out3, low3 = fix_z(c3, zr3, 2, 16, 63.0)
    for k, value in out2.items():
        c2[k, 0:24] = value
    c2[0, 0:24] = c2[0, 0:24] + low2
    for k, value in out3.items():
        c3[k] = value
    c3[0] = c3[0] + low3

    for h in range(2):
        total = c3[3 * h]
        for j in range(1, 3):
            if 3 * h + j < 5:
                total = total + roll(c3[3 * h + j], 40 * j)
        p3[h] = total
    g3[pl.ds(me, 1)] = p3[...][None]
    gather = []
    for d, device in enumerate(peers):
        c = pltpu.make_async_remote_copy(
            src_ref=p3, dst_ref=g3.at[me], send_sem=gsend.at[d], recv_sem=grecv.at[d],
            device_id=device, device_id_type=MESH,
        )
        c.start()
        gather.append(c)

    sets = ((c1, y1, y1r, 17, 16, 3.0), (c2, y2, y2r, 9, 8, 15.0))
    for c, y, _, count, n, _ in sets:
        for j in range(count):
            for k, row in enumerate((2 * n + 1, n, 2 * n + 2)):
                y[k, j:j + 1] = c[j, row:row + 1]
    round_y = []
    for _, y, yr, _, _, _ in sets:
        round_y.append(copy(y.at[0:2], yr.at[0:2], down_y))
        round_y.append(copy(y.at[2], yr.at[2], up_y))
    top_y, low_y = gy == ny - 1, gy == 0
    for c in round_y:
        c.wait_recv()
    for c, y, yr, count, n, factor in sets:
        rim = y[2]
        same_up = jnp.where(top_y, factor * rim, yr[0])
        plus_up = jnp.where(top_y, rim, yr[1])
        low = jnp.where(low_y, 0.0, yr[2])
        first = jnp.where(low_y, 0.0, y[1] - low)
        for j in range(count):
            c[j, n - 1:n] = c[j, n - 1:n] + same_up[j:j + 1]
            c[j, 2 * n:2 * n + 1] = c[j, 2 * n:2 * n + 1] + plus_up[j:j + 1]
            c[j, 0:1] = c[j, 0:1] + low[j:j + 1]
            c[j, n:n + 1] = first[j:j + 1]

    top_x, low_x = gx == nx - 1, gx == 0
    sets = ((c1, px1, px1r, t1, x1, 17, 40, 64, 3.0), (c2, px2, px2r, t2, x2, 9, 24, 32, 15.0))
    round_x = []
    for c, px, pxr, _, _, count, rows, n, _ in sets:
        lane = lax.broadcasted_iota(jnp.int32, (rows, 128), 1)
        total = None
        for j in range(count):
            if n == 64:
                part = roll(c[j, 0:rows, 128:256], j)
            else:
                part = roll(jnp.where(lane >= 64, c[j, 0:rows], 0.0), 64 + j)
            total = part if total is None else total + part
        px[...] = total
        round_x.append(copy(px, pxr.at[0], down_x))
        round_x.append(copy(px, pxr.at[1], up_x))
    for c in round_x:
        c.wait_recv()
    for c, px, pxr, t, x, count, rows, n, factor in sets:
        lane = lax.broadcasted_iota(jnp.int32, (rows, 128), 1)
        own = px[...]
        edge = jnp.where(lane < n // 2, factor * roll(own, -(n // 2)), roll(own, n // 2))
        above = jnp.where(top_x, edge, pxr[0])
        below = jnp.where(low_x, 0.0, pxr[1])
        x[...] = jnp.where(low_x, 0.0, own - roll(below, n // 2))
        at_end = (lane == n - 1) | (lane == 2 * n - 1)
        for j in range(count):
            value = c[j, 0:rows, 0:128]
            value = value + jnp.where(at_end, roll(above, n - 1 - j), 0.0)
            t[j] = value + jnp.where(lane == 0, roll(below, -(n // 2) - j), 0.0)

    for c in gather:
        c.wait()
    for c in raw + round_y + round_x:
        c.wait_send()


def expand_kernel(t1, x1, t2, x2, g3, qx, qy, o1, o2, o3, q3, s3):
    blocks = [[g3[4 * by + bx].reshape(32, 128) for by in range(4)] for bx in range(4)]
    left = []
    for bx in range(4):
        left += split(jnp.concatenate(blocks[bx], axis=0))
    q3[...] = dot(jnp.concatenate(left, axis=1), qx[...])
    for h in range(2):
        rows = jnp.concatenate(
            [q3[32 * by + 16 * h:32 * by + 16 * h + 16, :] for by in range(4)], axis=0
        )
        placed = dot(qy[...], jnp.concatenate(split(rows), axis=0))
        for j in range(3):
            if 3 * h + j < 5:
                s3[3 * h + j] = placed[0:40, 128 * j:128 * j + 128]

    def expand(t, x, o, nz, ny, n):
        def planes(k):
            value = t[k]
            lane = lax.broadcasted_iota(jnp.int32, value.shape, 1)
            first = 0.0 if x is None else roll(x[...], -(n + k))
            low = jnp.where(lane == 0, first, roll(value, 1 - n))
            return (low, value, roll(value, -n))

        for k in range(2 * nz + 1):
            for c, plane in enumerate(planes(k)):
                plane = plane[:, 0:n]
                if k < nz:
                    targets = [(1, k)]
                else:
                    targets = [(0, k - nz)] if k - nz < nz else []
                    targets += [(2, k - nz - 1)] if k > nz else []
                for a, layer in targets:
                    o[9 * a + c, layer] = plane[ny:2 * ny]
                    o[9 * a + 3 + c, layer] = plane[0:ny]
                    o[9 * a + 6 + c, layer] = plane[ny + 1:2 * ny + 1]

    expand(s3, None, o3, 2, 16, 64)
    expand(t2, x2, o2, 4, 8, 32)
    expand(t1, x1, o1, 8, 16, 64)


def shards(coeff_z, coeff_y, coeff_x, reaction):
    consts = []
    for level, rows in ((1, 48), (2, 32), (3, 16)):
        consts += weights_y(level, 32, rows)
    for level in (1, 2, 3):
        consts.append(weights_x(level, 128))
    vmem = pl.BlockSpec(memory_space=pltpu.VMEM)
    shape = jax.ShapeDtypeStruct
    v = pltpu.VMEM
    t1, x1, t2, x2, g3 = pl.pallas_call(
        main_kernel,
        out_shape=(
            shape((17, 40, 128), F32), shape((40, 128), F32),
            shape((9, 24, 128), F32), shape((24, 128), F32),
            shape((16, 2, 16, 128), F32),
        ),
        in_specs=[vmem] * 13,
        out_specs=(vmem,) * 5,
        scratch_shapes=[
            v((128, 17 * 128), BF16), v((64, 17 * 128), BF16),
            v((128, 11 * 128), BF16), v((64, 11 * 128), BF16),
            v((128, 7 * 128), BF16), v((64, 7 * 128), BF16),
            v((17, 48, 256), F32), v((11, 32, 128), F32), v((7, 16, 128), F32),
            v((4, 32, 128), F32), v((32, 128), F32), v((3, 24, 128), F32), v((3, 16, 128), F32),
            v((3, 24, 256), F32), v((3, 24, 256), F32), v((3, 16, 128), F32), v((3, 16, 128), F32),
            v((40, 128), F32), v((2, 40, 128), F32), v((24, 128), F32), v((2, 24, 128), F32),
            v((2, 16, 128), F32),
            pltpu.SemaphoreType.DMA((19,)), pltpu.SemaphoreType.DMA((19,)),
            pltpu.SemaphoreType.DMA((15,)), pltpu.SemaphoreType.DMA((15,)),
        ],
        compiler_params=pltpu.CompilerParams(
            collective_id=0, has_side_effects=True, vmem_limit_bytes=32 << 20
        ),
    )(reaction, coeff_z, coeff_y, coeff_x, *map(jnp.asarray, consts))
    return pl.pallas_call(
        expand_kernel,
        out_shape=(
            shape((27, 8, 16, 64), F32), shape((27, 4, 8, 32), F32), shape((27, 2, 16, 64), F32),
        ),
        in_specs=[vmem] * 7,
        out_specs=(vmem,) * 3,
        scratch_shapes=[v((128, 384), F32), v((5, 40, 128), F32)],
        compiler_params=pltpu.CompilerParams(vmem_limit_bytes=32 << 20),
    )(t1, x1, t2, x2, g3, jnp.asarray(place_x(4, 16)), jnp.asarray(place_y(4, 4, 48, 16)))


def solution(mesh):
    in_specs = (P("gz", "gy", "gx"),) * 4
    out_specs = (P(None, "gz", "gy", "gx"), P(None, "gz", "gy", "gx"), P(None, "gz", None, None))
    return jax.shard_map(shards, mesh=mesh, in_specs=in_specs, out_specs=out_specs, check_vma=False)
```

time: 680 us -> 35.8 us (0.05); the launches traced: 671 us -> 35.2 us
  local copies, waits for them, and re-layouts: 344 us -> 11.5 us
  other arithmetic: 188 us -> 0 us
  waiting for transfers between devices: 91.2 us -> 0 us
  starting transfers between devices: 23.4 us -> 0 us
  Pallas kernels: 0 us -> 23.1 us
  between operations: 15 us -> 0.68 us
  loops' own time: 9.05 us -> 0 us
    slice x59 -> x0, local copies, waits for them, and re-layouts: 261 us -> none  [the longest x18 87.4 us: restrict_axis(): upper = lax.slice_in_dim(field, 2, length + 1, 2, axis)]
    select_n x81 -> x0, other arithmetic: 102 us -> none  [the longest x9 89.3 us: colour_block(): image = jnp.where(inside[None], apply_fn(field, count), 0.0)]
    all_gather x1 -> x0, waiting for transfers between devices: 56.5 us -> none  [shards(): blocks = lax.all_gather(level_two[None], ('gy', 'gx'), axis=0, tiled=True)]
    mul x15 -> x0, local copies, waits for them, and re-layouts: 36.5 us -> none  [the longest x12 27 us: stencil_apply(): window(padded[offset:offset + 1], (1, 1, 1), count)]
    ppermute x10 -> x0, waiting for transfers between devices: 34.6 us -> none  [the longest x4 31.2 us: shifted(): return lax.ppermute(block, axis, route)]
    add x25 -> x0, other arithmetic: 26.7 us -> none  [the longest x18 26.7 us: restrict_axis(): return 0.5 * lower + middle + 0.5 * upper]
    concatenate x6 -> x0, other arithmetic: 23.4 us -> none  [the longest x2 11.7 us: with_halo(): block = jnp.concatenate([low, block, high], axis=dim)]
    ppermute x10 -> x0, starting transfers between devices: 23.3 us -> none  [the longest x3 13 us: with_halo(): lax.ppermute(lax.slice_in_dim(block, block.shape[dim] - width, None, axis...]
  transfers between devices with their start and end apart: 11 -> 0, of which waited for: 6 -> 0; matrix products, arithmetic and copies ran while one was open for 3% -> 0% of each run, Pallas kernels for 0% -> 0%
where the time goes in v1:
time: 35.8 us; the launch traced here: 35.2 us
  Pallas kernels  23.1 us (65%)
  local copies, waits for them, and re-layouts  11.5 us (32%)
  between operations  0.68 us (2%)
    pallas_call x1, Pallas kernels, shards(): pl.pallas_call(main_kernel, out_shape=(shape((17, 40, 128), F32), shape((...  21.1 us
    unnamed x30, local copies, waits for them, and re-layouts  11.5 us
    pallas_call x1, Pallas kernels, shards(): pl.pallas_call(expand_kernel, out_shape=(shape((27, 8, 16, 64), F32), sha...  1.98 us

profile of v1, /device:TPU:1, one launch (start us, length us, event | category | flops | bytes accessed | tf_op | source)
XLA Modules:
  0.0 35.2 jit_solution(7142777060055828666)
XLA Ops:
  0.6 0.0 copy-start
  0.6 0.0 copy-start.1
  0.7 1.0 %copy-done.1 = f32[16,32,128]{2,1,0:T(8,128)S(1)} copy-done((f32[16,32,128]{2,1,0:T(8,128)S(1)}, f32[16,32,128]{2,1,0:T(8,128)}, u32[]{:S(2)}) %copy-start.1) | copy-done | bytes 262168
  1.7 0.0 copy-start.2
  1.7 0.9 %copy-done.2 = f32[16,32,128]{2,1,0:T(8,128)S(1)} copy-done((f32[16,32,128]{2,1,0:T(8,128)S(1)}, f32[16,32,128]{2,1,0:T(8,128)}, u32[]{:S(2)}) %copy-start.2) | copy-done | bytes 262168
  2.6 0.0 copy-start.3
  2.6 0.9 %copy-done.3 = f32[16,32,128]{2,1,0:T(8,128)S(1)} copy-done((f32[16,32,128]{2,1,0:T(8,128)S(1)}, f32[16,32,128]{2,1,0:T(8,128)}, u32[]{:S(2)}) %copy-start.3) | copy-done | bytes 262168
  3.6 0.0 copy-start.4
  3.6 0.9 %copy-done.4 = f32[16,32,128]{2,1,0:T(8,128)S(1)} copy-done((f32[16,32,128]{2,1,0:T(8,128)S(1)}, f32[16,32,128]{2,1,0:T(8,128)}, u32[]{:S(2)}) %copy-start.4) | copy-done | bytes 262168
  4.5 0.0 copy-start.5
  4.5 0.9 %copy-done.5 = bf16[512,256]{1,0:T(8,128)(2,1)S(1)} copy-done((bf16[512,256]{1,0:T(8,128)(2,1)S(1)}, bf16[512,256]{1,0:T(8,128)(2,1)}, u32[]{:S(2)}) %copy-start.5) | copy-done | bytes 262168
  5.5 0.0 copy-start.6
  5.5 0.9 %copy-done.6 = bf16[512,128]{1,0:T(8,128)(2,1)S(1)} copy-done((bf16[512,128]{1,0:T(8,128)(2,1)S(1)}, bf16[512,128]{1,0:T(8,128)(2,1)}, u32[]{:S(2)}) %copy-start.6) | copy-done | bytes 131096
  6.4 0.0 copy-start.7
  6.4 0.9 %copy-done.7 = bf16[512,128]{1,0:T(8,128)(2,1)S(1)} copy-done((bf16[512,128]{1,0:T(8,128)(2,1)S(1)}, bf16[512,128]{1,0:T(8,128)(2,1)}, u32[]{:S(2)}) %copy-start.7) | copy-done | bytes 131096
  7.3 0.0 copy-start.9
  7.3 0.7 %copy-done.9 = bf16[48,64]{1,0:T(8,128)(2,1)S(1)} copy-done((bf16[48,64]{1,0:T(8,128)(2,1)S(1)}, bf16[48,64]{1,0:T(8,128)(2,1)}, u32[]{:S(2)}) %copy-start.9) | copy-done | bytes 6168
  8.0 0.0 copy-start.10
  8.0 0.7 %copy-done.10 = bf16[48,128]{1,0:T(8,128)(2,1)S(1)} copy-done((bf16[48,128]{1,0:T(8,128)(2,1)S(1)}, bf16[48,128]{1,0:T(8,128)(2,1)}, u32[]{:S(2)}) %copy-start.10) | copy-done | bytes 12312
  8.7 0.0 copy-start.11
  8.7 0.7 %copy-done.11 = bf16[32,64]{1,0:T(8,128)(2,1)S(1)} copy-done((bf16[32,64]{1,0:T(8,128)(2,1)S(1)}, bf16[32,64]{1,0:T(8,128)(2,1)}, u32[]{:S(2)}) %copy-start.11) | copy-done | bytes 4120
  9.4 0.0 copy-start.12
  9.4 0.7 %copy-done.12 = bf16[32,128]{1,0:T(8,128)(2,1)S(1)} copy-done((bf16[32,128]{1,0:T(8,128)(2,1)S(1)}, bf16[32,128]{1,0:T(8,128)(2,1)}, u32[]{:S(2)}) %copy-start.12) | copy-done | bytes 8216
  10.1 0.0 copy-start.13
  10.1 0.7 %copy-done.13 = bf16[16,64]{1,0:T(8,128)(2,1)S(1)} copy-done((bf16[16,64]{1,0:T(8,128)(2,1)S(1)}, bf16[16,64]{1,0:T(8,128)(2,1)}, u32[]{:S(2)}) %copy-start.13) | copy-done | bytes 2072
  10.8 0.0 copy-start.14
  10.8 0.7 %copy-done.14 = bf16[16,128]{1,0:T(8,128)(2,1)S(1)} copy-done((bf16[16,128]{1,0:T(8,128)(2,1)S(1)}, bf16[16,128]{1,0:T(8,128)(2,1)}, u32[]{:S(2)}) %copy-start.14) | copy-done | bytes 4120
  11.5 21.1 %shard_map.166 = (f32[17,40,128]{2,1,0:T(8,128)S(1)}, f32[40,128]{1,0:T(8,128)S(1)}, f32[9,24,128]{2,1,0:T(8,128)S(1)}, f32[24,128]{1,0:T(8,128)S(1)}, f32[16,2,16,128]{3,2,1,0:T(8,128)S(1)}) custom-call(f32[16,32,128]{2,1,0:T(8,128)S(1)} %copy-done.1, f32[16,32,128]{2,1,0:T(8,128)S(1)} %copy-done.2, f32[16,32,128]{2,1,0:T(8,128)S(1)} %copy-done.3, ...), custom_call_target="tpu_custom_call" | custom-call | tf_op jit(solution)/shard_map/pallas_call | solution.py:442
  32.6 0.0 copy-done
  32.6 0.0 copy-start.8
  32.6 0.7 %copy-done.8 = bf16[48,128]{1,0:T(8,128)(2,1)S(1)} copy-done((bf16[48,128]{1,0:T(8,128)(2,1)S(1)}, bf16[48,128]{1,0:T(8,128)(2,1)}, u32[]{:S(2)}) %copy-start.8) | copy-done | bytes 12312
  33.3 2.0 %shard_map.167 = (f32[27,8,16,64]{3,2,1,0:T(8,128)}, f32[27,4,8,32]{3,2,1,0:T(8,128)}, f32[27,2,16,64]{3,2,1,0:T(8,128)}) custom-call(f32[17,40,128]{2,1,0:T(8,128)S(1)} %get-tuple-element.8.t1, f32[40,128]{1,0:T(8,128)S(1)} %get-tuple-element.9.x1, f32[9,24,128]{2,1,0:T(8,128)S(1)} %get-tuple-element.10.t2, f32[24,128]{1,0:T(8,128)S(1)} %get-tuple-element.11.x2, ...), custom_call_target="tpu_custom_call" | custom-call | tf_op jit(solution)/shard_map/pallas_call | solution.py:467
Async XLA Ops:
  0.6 31.9 %copy-start = (bf16[1024,384]{1,0:T(8,128)(2,1)S(1)}, bf16[1024,384]{1,0:T(8,128)(2,1)}, u32[]{:S(2)}) copy-start(bf16[1024,384]{1,0:T(8,128)(2,1)} %constant.31.clone.qx) | copy-start | bytes 2359300
  0.6 1.0 %copy-start.1 = (f32[16,32,128]{2,1,0:T(8,128)S(1)}, f32[16,32,128]{2,1,0:T(8,128)}, u32[]{:S(2)}) copy-start(f32[16,32,128]{2,1,0:T(8,128)} %r_ref.1) | copy-start | bytes 786436
  1.7 0.9 %copy-start.2 = (f32[16,32,128]{2,1,0:T(8,128)S(1)}, f32[16,32,128]{2,1,0:T(8,128)}, u32[]{:S(2)}) copy-start(f32[16,32,128]{2,1,0:T(8,128)} %kz_ref.1) | copy-start | bytes 786436
  2.6 0.9 %copy-start.3 = (f32[16,32,128]{2,1,0:T(8,128)S(1)}, f32[16,32,128]{2,1,0:T(8,128)}, u32[]{:S(2)}) copy-start(f32[16,32,128]{2,1,0:T(8,128)} %ky_ref.1) | copy-start | bytes 786436
  3.6 0.9 %copy-start.4 = (f32[16,32,128]{2,1,0:T(8,128)S(1)}, f32[16,32,128]{2,1,0:T(8,128)}, u32[]{:S(2)}) copy-start(f32[16,32,128]{2,1,0:T(8,128)} %kx_ref.1) | copy-start | bytes 786436
  4.5 0.9 %copy-start.5 = (bf16[512,256]{1,0:T(8,128)(2,1)S(1)}, bf16[512,256]{1,0:T(8,128)(2,1)}, u32[]{:S(2)}) copy-start(bf16[512,256]{1,0:T(8,128)(2,1)} %constant.28.clone.wx1) | copy-start | bytes 786436
  5.5 0.9 %copy-start.6 = (bf16[512,128]{1,0:T(8,128)(2,1)S(1)}, bf16[512,128]{1,0:T(8,128)(2,1)}, u32[]{:S(2)}) copy-start(bf16[512,128]{1,0:T(8,128)(2,1)} %constant.30.clone.wx3) | copy-start | bytes 393220
  6.4 0.9 %copy-start.7 = (bf16[512,128]{1,0:T(8,128)(2,1)S(1)}, bf16[512,128]{1,0:T(8,128)(2,1)}, u32[]{:S(2)}) copy-start(bf16[512,128]{1,0:T(8,128)(2,1)} %constant.29.clone.wx2) | copy-start | bytes 393220
  7.3 0.7 %copy-start.9 = (bf16[48,64]{1,0:T(8,128)(2,1)S(1)}, bf16[48,64]{1,0:T(8,128)(2,1)}, u32[]{:S(2)}) copy-start(bf16[48,64]{1,0:T(8,128)(2,1)} %constant.23.clone.wy1b) | copy-start | bytes 18436
  8.0 0.7 %copy-start.10 = (bf16[48,128]{1,0:T(8,128)(2,1)S(1)}, bf16[48,128]{1,0:T(8,128)(2,1)}, u32[]{:S(2)}) copy-start(bf16[48,128]{1,0:T(8,128)(2,1)} %constant.22.clone.wy1a) | copy-start | bytes 36868
  8.7 0.7 %copy-start.11 = (bf16[32,64]{1,0:T(8,128)(2,1)S(1)}, bf16[32,64]{1,0:T(8,128)(2,1)}, u32[]{:S(2)}) copy-start(bf16[32,64]{1,0:T(8,128)(2,1)} %constant.25.clone.wy2b) | copy-start | bytes 12292
  9.4 0.7 %copy-start.12 = (bf16[32,128]{1,0:T(8,128)(2,1)S(1)}, bf16[32,128]{1,0:T(8,128)(2,1)}, u32[]{:S(2)}) copy-start(bf16[32,128]{1,0:T(8,128)(2,1)} %constant.24.clone.wy2a) | copy-start | bytes 24580
  10.1 0.7 %copy-start.13 = (bf16[16,64]{1,0:T(8,128)(2,1)S(1)}, bf16[16,64]{1,0:T(8,128)(2,1)}, u32[]{:S(2)}) copy-start(bf16[16,64]{1,0:T(8,128)(2,1)} %constant.27.clone.wy3b) | copy-start | bytes 6148
  10.8 0.7 %copy-start.14 = (bf16[16,128]{1,0:T(8,128)(2,1)S(1)}, bf16[16,128]{1,0:T(8,128)(2,1)}, u32[]{:S(2)}) copy-start(bf16[16,128]{1,0:T(8,128)(2,1)} %constant.26.clone.wy3a) | copy-start | bytes 12292
  32.6 0.7 %copy-start.8 = (bf16[48,128]{1,0:T(8,128)(2,1)S(1)}, bf16[48,128]{1,0:T(8,128)(2,1)}, u32[]{:S(2)}) copy-start(bf16[48,128]{1,0:T(8,128)(2,1)} %constant.32.clone.qy) | copy-start | bytes 36868

commit v2 on v1

v2 whole, which is shorter than its diff:
```python
from functools import partial

import jax
import jax.numpy as jnp
import ml_dtypes
import numpy as np
from jax import lax
from jax.experimental import pallas as pl
from jax.experimental.pallas import tpu as pltpu
from jax.sharding import PartitionSpec as P

MESH = pl.DeviceIdType.MESH
F32 = jnp.float32
BF16 = jnp.bfloat16


def forms(level, n):
    step = 1 << level
    i = np.arange(n)

    def hat(i, index):
        return np.maximum(0.0, 1.0 - np.abs(i - (step * index + step - 1)) / step)

    def slope(i, index):
        return hat(i, index) - hat(i + 1, index)

    def column(plus, index):
        other = index + plus
        return hat(i, index) * hat(i, other), slope(i, index) * slope(i, other)

    return column


def row_order(count):
    return (
        [(0, j) for j in range(count)]
        + [(1, j) for j in range(-1, count)]
        + [(0, -1), (0, count)]
    )


def y_rows(level, count):
    order = row_order(count)
    if level == 3:
        return dict(zip(order, range(len(order))))
    place = {(0, j): j for j in range(count)}
    place.update({(1, j): count + 8 + j for j in range(count)})
    place.update({(0, -1): count + 5, (0, count): count + 6, (1, -1): count + 7})
    return place


def weights_y(level, n, rows):
    column = forms(level, n)
    mass = np.zeros((rows, n))
    stiff = np.zeros((rows, n))
    for (plus, index), row in y_rows(level, n >> level).items():
        mass[row], stiff[row] = column(plus, index)
    first = np.concatenate([mass, mass, stiff, stiff], axis=1)
    second = np.concatenate([mass, mass], axis=1)
    return first, second


def lanes_of(level, n):
    count = n >> level
    if level == 3:
        return [(0, j) for j in range(-1, count + 1)] + [(1, j) for j in range(-1, count)], 128
    rim = 2 * count
    lanes = [(0, j) for j in range(count)] + [(1, j) for j in range(count)]
    lanes += [None] * (2 * count)
    lanes[rim] = (0, -1)
    lanes[rim + count // 2] = (0, count)
    lanes[rim + count] = (1, -1)
    return lanes, 4 * count


def weights_x(level, n):
    column = forms(level, n)
    lanes, width = lanes_of(level, n)
    mass = np.zeros((n, width))
    stiff = np.zeros((n, width))
    for lane, entry in enumerate(lanes):
        if entry is not None:
            mass[:, lane], stiff[:, lane] = column(*entry)
    scale = 0.5**level
    both = np.concatenate([mass, mass, stiff, stiff], axis=0) * scale
    return both


def place_x(blocks, count):
    whole = blocks * count
    out = np.zeros((blocks, 2, 128, 3 * 128))
    for block in range(blocks):
        for layer in range(3):
            entries = lanes_of(3, count * 8)[0]
            for lane, (plus, index) in enumerate(entries):
                source = 40 * layer + lane
                target = block * count + index
                if 0 <= target < whole:
                    out[block, :, source, layer * 128 + plus * whole + target] = 1.0
                if plus == 0 and target == whole:
                    out[block, :, source, layer * 128 + whole - 1] = 63.0
                    out[block, :, source, layer * 128 + 2 * whole - 1] = 1.0
    return out.reshape(blocks * 256, 384).astype(ml_dtypes.bfloat16)


def place_y(blocks, count, rows, packed):
    whole = blocks * count
    out = np.zeros((rows, 2, blocks, packed))
    for block in range(blocks):
        for row, (plus, index) in enumerate(row_order(count)):
            target = block * count + index
            if 0 <= target < whole:
                out[target + plus * (whole + 8), :, block, row] = 1.0
            if plus == 0 and target == whole:
                out[whole - 1, :, block, row] = 63.0
                out[2 * whole + 7, :, block, row] = 1.0
    return out.reshape(rows, 2 * blocks * packed).astype(ml_dtypes.bfloat16)


def split(value):
    high = value.astype(BF16)
    return high, (value - high.astype(F32)).astype(BF16)


def dot(left, right):
    return jnp.dot(left, right, preferred_element_type=F32)


def roll(value, shift):
    return pltpu.roll(value, shift % 128, 1)


def mass_layers(field):
    n = len(field)
    quarter = [0.25 * field[2 * j] for j in range(n // 2)] + [None]
    same = {-1: quarter[0]}
    plus = {-1: quarter[0]}
    for j in range(n // 2):
        total = field[2 * j + 1] + quarter[j]
        same[j] = total if quarter[j + 1] is None else total + quarter[j + 1]
        plus[j] = quarter[j + 1]
    same[n // 2] = None
    return same, plus


def stiff_layers(field):
    n = len(field)
    share = {-1: 0.25 * field[0], n // 2 - 1: 0.25 * field[n - 1]}
    for j in range(n // 2 - 1):
        share[j] = 0.25 * (field[2 * j + 1] + field[2 * j + 2])
    same = {-1: share[-1], n // 2: share[n // 2 - 1]}
    for j in range(n // 2):
        same[j] = share[j - 1] + share[j]
    return same, share


def plus_of(a, b):
    if a is None:
        return b
    return a if b is None else a + b


def coarser(same, plus, count):
    def scaled(value, factor):
        return None if value is None else factor * value

    new_same, new_plus = {}, {}
    half = count // 2
    for j in range(-1, half + 1):
        total = scaled(plus_of(same.get(2 * j), same.get(2 * j + 2)), 0.25)
        for term in (same.get(2 * j + 1), plus.get(2 * j), plus.get(2 * j + 1)):
            total = plus_of(total, term)
        new_same[j] = total
    for j in range(-1, half):
        total = scaled(plus_of(plus.get(2 * j + 1), plus.get(2 * j + 2)), 0.5)
        new_plus[j] = plus_of(total, scaled(same.get(2 * j + 2), 0.25))
    return new_same, new_plus


def all_weights():
    out = np.zeros((576, 512))
    for level, start, width in ((1, 0, 256), (2, 256, 128), (3, 384, 128)):
        out[:512, start:start + width] = weights_x(level, 128)
    for level, row, rows, lane in ((1, 512, 48, 0), (2, 512, 32, 256), (3, 560, 16, 0)):
        first, second = weights_y(level, 32, rows)
        out[row:row + rows, lane:lane + 128] = first
        out[row:row + rows, lane + 128:lane + 192] = second
    return out.astype(ml_dtypes.bfloat16)


def main_kernel(
    r_hbm, kz_hbm, ky_hbm, kx_hbm, w_hbm,
    t1, x1, t2, x2, g3,
    f4, w, zs, zu, zl, rims, rimr,
    ga1, gb1, ga2, gb2, ga3, gb3, c2, c3,
    yb, yr, px, pxr, pxf, dr, p3,
    lsem, send, recv, gsend, grecv,
):
    gz, gy, gx = lax.axis_index("gz"), lax.axis_index("gy"), lax.axis_index("gx")
    nz, ny, nx = lax.axis_size("gz"), lax.axis_size("gy"), lax.axis_size("gx")
    zp, zm = lax.rem(gz + 1, nz), lax.rem(gz + nz - 1, nz)
    yp, ym = lax.rem(gy + 1, ny), lax.rem(gy + ny - 1, ny)
    xp, xm = lax.rem(gx + 1, nx), lax.rem(gx + nx - 1, nx)
    slab = ny * nx
    me = gy * nx + gx
    peers = []
    for d in range(1, slab):
        t = lax.rem(me + d, slab)
        peers.append((gz, lax.div(t, nx), lax.rem(t, nx)))

    barrier = pltpu.get_barrier_semaphore()
    for device in [(zp, gy, gx), (zm, gy, gx)] + peers:
        pl.semaphore_signal(barrier, inc=1, device_id=device, device_id_type=MESH)

    fields = (r_hbm, kz_hbm, ky_hbm, kx_hbm)
    first = [pltpu.make_async_copy(f.at[0], zs.at[j], lsem.at[j]) for j, f in enumerate(fields)]
    first.append(pltpu.make_async_copy(kz_hbm.at[15], zs.at[4], lsem.at[4]))
    bulk = [pltpu.make_async_copy(f, f4.at[j], lsem.at[5 + j]) for j, f in enumerate(fields)]
    bulk.append(pltpu.make_async_copy(w_hbm, w, lsem.at[9]))
    for c in first + bulk:
        c.start()

    started = []

    def copy(src, dst, device):
        k = len(started)
        c = pltpu.make_async_remote_copy(
            src_ref=src, dst_ref=dst, send_sem=send.at[k], recv_sem=recv.at[k],
            device_id=device, device_id_type=MESH,
        )
        c.start()
        started.append(c)
        return c

    for c in first:
        c.wait()
    pl.semaphore_wait(barrier, slab + 1)
    raw = [copy(zs.at[0:4], zu, (zm, gy, gx)), copy(zs.at[4], zl, (zp, gy, gx))]
    for c in bulk:
        c.wait()

    def layers(j):
        return [f4[j, k] for k in range(16)]

    same1, plus1 = mass_layers(layers(0))
    ssame, share = stiff_layers(layers(1))
    for j in range(-1, 9):
        same1[j] = plus_of(same1[j], ssame[j])
    for j in range(-1, 8):
        plus1[j] = -share[j] if plus1[j] is None else plus1[j] - share[j]
    level1 = [(same1, plus1), mass_layers(layers(2)), mass_layers(layers(3))]
    level2 = [coarser(*f, 8) for f in level1]
    level3 = [coarser(*f, 4) for f in level2]

    zero = jnp.zeros((32, 128), F32)

    def put(ga, gb, j, values):
        lanes = pl.ds(128 * j, 128)
        for base, (ref, value) in enumerate(zip((ga, ga, gb), values)):
            high, low = split(zero if value is None else value)
            start = 64 * base if base < 2 else 0
            ref[start:start + 32, lanes] = high
            ref[start + 32:start + 64, lanes] = low

    def reduce_yx(ga, gb, wya, wyb, wx, start, count, rows):
        lanes = pl.ds(128 * start, 128 * count)
        left = []
        for value in (dot(wya, ga[:, lanes]), dot(wyb, gb[:, lanes])):
            stacked = jnp.concatenate(
                [value[:, 128 * j:128 * j + 128] for j in range(count)], axis=0
            )
            left += split(stacked)
        out = dot(jnp.concatenate(left, axis=1), wx)
        return [out[rows * j:rows * j + rows] for j in range(count)]

    for j, (plus, index) in enumerate(row_order(2)):
        put(ga3, gb3, j, [f[plus][index] for f in level3])
    for j, (plus, index) in enumerate(row_order(4)):
        put(ga2, gb2, j, [f[plus][index] for f in level2])
    out3 = reduce_yx(
        ga3, gb3, w[560:576, 0:128], w[560:576, 128:192], w[0:512, 384:512], 0, 7, 16
    )
    out2 = reduce_yx(
        ga2, gb2, w[512:544, 256:384], w[512:544, 384:448], w[0:512, 256:384], 0, 11, 32
    )
    for k, (j3, j2) in enumerate(((5, 9), (2, 4), (6, 10))):
        rims[k, 0:24] = out2[j2][0:24]
        rims[k, 24:40] = out3[j3]
    for j in range(9):
        c2[j] = out2[j][0:24]
    for j in range(5):
        c3[j] = out3[j]
    round_z = [
        copy(rims.at[0:2], rimr.at[0:2], (zm, gy, gx)),
        copy(rims.at[2], rimr.at[2], (zp, gy, gx)),
    ]

    order1 = row_order(8)
    inner = list(range(1, 7)) + list(range(9, 16))
    outer = [0, 7, 8, 16]
    x_total = [None, None]

    def level_one(start, places):
        for j, k in enumerate(places):
            plus, index = order1[k]
            put(ga1, gb1, start + j, [f[plus][index] for f in level1])
        out = reduce_yx(
            ga1, gb1, w[512:560, 0:128], w[512:560, 128:192], w[0:512, 0:256],
            start, len(places), 48,
        )
        for k, value in zip(places, out):
            t1[k] = value[0:40, 0:128]
            x_total[0] = plus_of(x_total[0], roll(value[0:40, 128:256], k))
            for slot, row in ((0, 21), (1, 23), (3, 22)):
                yb[slot, k:k + 1] = value[row:row + 1, 0:128]

    level_one(0, inner)

    top_z, low_z = gz == nz - 1, gz == 0
    for c in raw:
        c.wait_recv()
    last = share[7]
    up_r, up_kz = 0.25 * zu[0], 0.25 * zu[1]
    up_ky, up_kx = 0.25 * zu[2], 0.25 * zu[3]
    come = jnp.where(low_z, 0.0, 0.25 * zl[...])
    add_same = [jnp.where(top_z, 3.0 * last, up_r + up_kz)]
    add_plus = [jnp.where(top_z, last, up_r - up_kz)]
    for f in (up_ky, up_kx):
        add_same.append(jnp.where(top_z, 0.0, f))
        add_plus.append(add_same[-1])
    for f in range(3):
        same, plus = level1[f]
        same[7] = plus_of(same[7], add_same[f])
        plus[7] = plus_of(plus[7], add_plus[f])
        if f == 0:
            same[0] = same[0] + come
            plus[-1] = plus[-1] - come
        plus[-1] = jnp.where(low_z, 0.0, plus[-1])
    level_one(13, outer)

    for c in round_z:
        c.wait_recv()
    rim = rims[2]
    factor = jnp.where(lax.broadcasted_iota(jnp.int32, (40, 128), 0) < 24, 15.0, 63.0)
    same_up = jnp.where(top_z, factor * rim, rimr[0])
    plus_up = jnp.where(top_z, rim, rimr[1])
    low = jnp.where(low_z, 0.0, rimr[2])
    fix2 = {0: low, 3: same_up, 4: -low, 8: plus_up}
    fix3 = {0: low, 1: same_up, 2: -low, 4: plus_up}
    lane2 = lax.broadcasted_iota(jnp.int32, (24, 128), 1)
    for j in range(9):
        value = c2[j] if j not in fix2 else c2[j] + fix2[j][0:24]
        if j == 4:
            value = jnp.where(low_z, 0.0, value)
        t2[j] = value
        x_total[1] = plus_of(x_total[1], roll(jnp.where(lane2 >= 64, value, 0.0), 64 + j))
        for slot, row in ((0, 13), (1, 15), (3, 14)):
            yb[slot, 24 + j:25 + j] = value[row:row + 1]
    packed = [None, None]
    for j in range(5):
        value = c3[j] if j not in fix3 else c3[j] + fix3[j][24:40]
        if j == 2:
            value = jnp.where(low_z, 0.0, value)
        packed[j // 3] = plus_of(packed[j // 3], roll(value, 40 * (j % 3)) if j % 3 else value)

    px[0:40] = x_total[0]
    px[40:64] = x_total[1]
    yb[2, 0:8] = x_total[0][16:24]
    yb[2, 8:16] = x_total[1][8:16]
    p3[0] = packed[0]
    p3[1] = packed[1]
    round_yx = [
        copy(px, pxr.at[0], (gz, gy, xm)),
        copy(px, pxr.at[1], (gz, gy, xp)),
        copy(yb.at[0:3], yr.at[0, 0:3], (gz, ym, gx)),
        copy(yb.at[2:4], yr.at[1, 2:4], (gz, yp, gx)),
        copy(yb.at[2, 0:16], dr.at[0], (gz, ym, xm)),
        copy(yb.at[2, 0:16], dr.at[1], (gz, ym, xp)),
        copy(yb.at[2, 0:16], dr.at[2], (gz, yp, xm)),
        copy(yb.at[2, 0:16], dr.at[3], (gz, yp, xp)),
    ]
    gather = []
    for d, device in enumerate(peers):
        c = pltpu.make_async_remote_copy(
            src_ref=p3, dst_ref=g3.at[me], send_sem=gsend.at[d], recv_sem=grecv.at[d],
            device_id=device, device_id_type=MESH,
        )
        c.start()
        gather.append(c)
    g3[pl.ds(me, 1)] = p3[...][None]

    top_y, low_y = gy == ny - 1, gy == 0
    top_x, low_x = gx == nx - 1, gx == 0
    for c in round_yx:
        c.wait_recv()

    for t, first, count, n, factor in ((t1, 0, 17, 16, 3.0), (t2, 24, 9, 8, 15.0)):
        span = slice(first, first + (24 if n == 16 else 16))
        rim = yb[3, span]
        same_up = jnp.where(top_y, factor * rim, yr[0, 0, span])
        plus_up = jnp.where(top_y, rim, yr[0, 1, span])
        low = jnp.where(low_y, 0.0, yr[1, 3, span])
        bottom = jnp.where(low_y, 0.0, yb[1, span] - low)
        for j in range(count):
            t[j, n - 1:n] = t[j, n - 1:n] + same_up[j:j + 1]
            t[j, 2 * n + 7:2 * n + 8] = t[j, 2 * n + 7:2 * n + 8] + plus_up[j:j + 1]
            t[j, 0:1] = t[j, 0:1] + low[j:j + 1]
            t[j, n + 7:n + 8] = bottom[j:j + 1]

    sources = (
        (px, yr.at[0, 2], yr.at[1, 2]),
        (pxr.at[0], dr.at[0], dr.at[2]),
        (pxr.at[1], dr.at[1], dr.at[3]),
    )
    for k, (source, upper, lower) in enumerate(sources):
        pxf[k] = source[...]
        for base, group, n, factor in ((0, 0, 16, 3.0), (40, 8, 8, 15.0)):
            rim = source[base + n + 6:base + n + 7]
            same_up = jnp.where(top_y, factor * rim, upper[group + 5:group + 6])
            plus_up = jnp.where(top_y, rim, upper[group + 7:group + 8])
            low = jnp.where(low_y, 0.0, lower[group + 6:group + 7])
            for row, value in ((n - 1, same_up), (2 * n + 7, plus_up), (0, low)):
                at = slice(base + row, base + row + 1)
                pxf[k, at] = pxf[k, at] + value
            at = slice(base + n + 7, base + n + 8)
            pxf[k, at] = jnp.where(low_y, 0.0, pxf[k, at] - low)

    sets = ((t1, x1, 17, 0, 40, 64, 3.0), (t2, x2, 9, 40, 24, 32, 15.0))
    for t, x, count, base, rows, n, factor in sets:
        lane = lax.broadcasted_iota(jnp.int32, (rows, 128), 1)
        own = pxf[0, base:base + rows]
        edge = jnp.where(lane < n // 2, factor * roll(own, -(n // 2)), roll(own, n // 2))
        above = jnp.where(top_x, edge, pxf[1, base:base + rows])
        below = jnp.where(low_x, 0.0, pxf[2, base:base + rows])
        x[...] = jnp.where(low_x, 0.0, own - roll(below, n // 2))
        at_end = (lane == n - 1) | (lane == 2 * n - 1)
        for j in range(count):
            value = t[j] + jnp.where(at_end, roll(above, n - 1 - j), 0.0)
            t[j] = value + jnp.where(lane == 0, roll(below, -(n // 2) - j), 0.0)

    for c in gather:
        c.wait()
    for c in started:
        c.wait_send()


def expand_kernel(
    t1, x1, t2, x2, g3, qx_hbm, qy_hbm, o1, o2, o3, qx, qy, q3, s3, v1, v2, v3, csem, osem
):
    consts = [
        pltpu.make_async_copy(qx_hbm, qx, csem.at[0]),
        pltpu.make_async_copy(qy_hbm, qy, csem.at[1]),
    ]
    for c in consts:
        c.start()
    pending = []

    def expand(t, x, v, o, nz, ny, n, order):
        done = [set() for _ in range(3)]
        rows = {0: slice(ny + 7, 2 * ny + 7), 1: slice(0, ny), 2: slice(ny + 8, 2 * ny + 8)}
        for k in order:
            value = t[k]
            lane = lax.broadcasted_iota(jnp.int32, value.shape, 1)
            first = 0.0 if x is None else roll(x[...], -(n + k))
            low = jnp.where(lane == 0, first, roll(value, 1 - n))
            planes = (low, value, roll(value, -n))
            if k < nz:
                targets = [(1, k)]
            else:
                targets = [(0, k - nz)] if k - nz < nz else []
                targets += [(2, k - nz - 1)] if k > nz else []
            for c, plane in enumerate(planes):
                plane = plane[:, 0:n]
                for a, layer in targets:
                    for b in range(3):
                        v[9 * a + 3 * b + c, layer] = plane[rows[b]]
            for a, layer in targets:
                done[a].add(layer)
                if len(done[a]) == nz:
                    part = pl.ds(9 * a, 9)
                    copy = pltpu.make_async_copy(v.at[part], o.at[part], osem.at[len(pending)])
                    copy.start()
                    pending.append(copy)

    expand(t1, x1, v1, o1, 8, 16, 64, range(17))
    expand(t2, x2, v2, o2, 4, 8, 32, range(9))

    for c in consts:
        c.wait()
    left = []
    for bx in range(4):
        blocks = [g3[4 * by + bx].reshape(32, 128) for by in range(4)]
        left += split(jnp.concatenate(blocks, axis=0))
    q3[...] = dot(jnp.concatenate(left, axis=1), qx[...])
    for h in range(2):
        rows = jnp.concatenate(
            [q3[32 * by + 16 * h:32 * by + 16 * h + 16, :] for by in range(4)], axis=0
        )
        placed = dot(qy[...], jnp.concatenate(split(rows), axis=0))
        for j in range(3):
            if 3 * h + j < 5:
                s3[3 * h + j] = placed[0:40, 128 * j:128 * j + 128]
    expand(s3, None, v3, o3, 2, 16, 64, range(5))
    for copy in pending:
        copy.wait()


def shards(coeff_z, coeff_y, coeff_x, reaction):
    vmem = pl.BlockSpec(memory_space=pltpu.VMEM)
    hbm = pl.BlockSpec(memory_space=pltpu.HBM)
    shape = jax.ShapeDtypeStruct
    v = pltpu.VMEM
    dma = pltpu.SemaphoreType.DMA
    t1, x1, t2, x2, g3 = pl.pallas_call(
        main_kernel,
        out_shape=(
            shape((17, 40, 128), F32), shape((40, 128), F32),
            shape((9, 24, 128), F32), shape((24, 128), F32),
            shape((16, 2, 16, 128), F32),
        ),
        in_specs=[hbm] * 5,
        out_specs=(vmem,) * 5,
        scratch_shapes=[
            v((4, 16, 32, 128), F32), v((576, 512), BF16),
            v((5, 32, 128), F32), v((4, 32, 128), F32), v((32, 128), F32),
            v((3, 40, 128), F32), v((3, 40, 128), F32),
            v((128, 17 * 128), BF16), v((64, 17 * 128), BF16),
            v((128, 11 * 128), BF16), v((64, 11 * 128), BF16),
            v((128, 7 * 128), BF16), v((64, 7 * 128), BF16),
            v((9, 24, 128), F32), v((5, 16, 128), F32),
            v((4, 40, 128), F32), v((2, 4, 40, 128), F32),
            v((64, 128), F32), v((2, 64, 128), F32), v((3, 64, 128), F32),
            v((4, 16, 128), F32), v((2, 16, 128), F32),
            dma((10,)), dma((12,)), dma((12,)), dma((15,)), dma((15,)),
        ],
        compiler_params=pltpu.CompilerParams(
            collective_id=0, has_side_effects=True, vmem_limit_bytes=62 << 20
        ),
    )(reaction, coeff_z, coeff_y, coeff_x, jnp.asarray(all_weights()))
    return pl.pallas_call(
        expand_kernel,
        out_shape=(
            shape((27, 8, 16, 64), F32), shape((27, 4, 8, 32), F32), shape((27, 2, 16, 64), F32),
        ),
        in_specs=[vmem] * 5 + [hbm] * 2,
        out_specs=(hbm,) * 3,
        scratch_shapes=[
            v((1024, 384), BF16), v((48, 128), BF16), v((128, 384), F32), v((5, 40, 128), F32),
            v((27, 8, 16, 64), F32), v((27, 4, 8, 32), F32), v((27, 2, 16, 64), F32),
            dma((2,)), dma((9,)),
        ],
        compiler_params=pltpu.CompilerParams(vmem_limit_bytes=62 << 20),
    )(t1, x1, t2, x2, g3, jnp.asarray(place_x(4, 16)), jnp.asarray(place_y(4, 4, 48, 16)))


def solution(mesh):
    in_specs = (P("gz", "gy", "gx"),) * 4
    out_specs = (P(None, "gz", "gy", "gx"), P(None, "gz", "gy", "gx"), P(None, "gz", None, None))
    return jax.shard_map(shards, mesh=mesh, in_specs=in_specs, out_specs=out_specs, check_vma=False)
```

time: 35.8 us -> 25.5 us (0.71); the launches traced: 35.2 us -> 25.3 us
  local copies, waits for them, and re-layouts: 11.5 us -> 0 us
  Pallas kernels: 23.1 us -> 24.7 us
    unnamed x30 -> x0, local copies, waits for them, and re-layouts: 11.5 us -> none
    pallas_call x1, Pallas kernels: 1.98 us -> 4.38 us  [shards(): pl.pallas_call(expand_kernel, out_shape=(shape((27, 8, 16, 64), F32), sha...]
    pallas_call x1, Pallas kernels: 21.1 us -> 20.3 us  [shards(): pl.pallas_call(main_kernel, out_shape=(shape((17, 40, 128), F32), shape((...]
where the time goes in v2:
time: 25.5 us; the launch traced here: 25.3 us
  Pallas kernels  24.7 us (97%)
  between operations  0.64 us (3%)
    pallas_call x1, Pallas kernels, shards(): pl.pallas_call(main_kernel, out_shape=(shape((17, 40, 128), F32), shape((...  20.3 us
    pallas_call x1, Pallas kernels, shards(): pl.pallas_call(expand_kernel, out_shape=(shape((27, 8, 16, 64), F32), sha...  4.38 us

profile of v2, /device:TPU:1, one launch (start us, length us, event | category | flops | bytes accessed | tf_op | source)
XLA Modules:
  0.0 25.3 jit_solution(11558063804715205329)
XLA Ops:
  0.6 20.3 %shard_map.94 = (f32[17,40,128]{2,1,0:T(8,128)}, f32[40,128]{1,0:T(8,128)}, f32[9,24,128]{2,1,0:T(8,128)}, f32[24,128]{1,0:T(8,128)}, f32[16,2,16,128]{3,2,1,0:T(8,128)}) custom-call(f32[16,32,128]{2,1,0:T(8,128)} %r_hbm.1, f32[16,32,128]{2,1,0:T(8,128)} %kz_hbm.1, f32[16,32,128]{2,1,0:T(8,128)} %ky_hbm.1, f32[16,32,128]{2,1,0:T(8,128)} %kx_hbm.1, ...), custom_call_target="tpu_custom_call" | custom-call | tf_op jit(solution)/shard_map/pallas_call | solution.py:514
  20.9 4.4 %shard_map.95 = (f32[27,8,16,64]{3,2,1,0:T(8,128)}, f32[27,4,8,32]{3,2,1,0:T(8,128)}, f32[27,2,16,64]{3,2,1,0:T(8,128)}) custom-call(f32[17,40,128]{2,1,0:T(8,128)} %get-tuple-element.8.t1, f32[40,128]{1,0:T(8,128)} %get-tuple-element.9.x1, f32[9,24,128]{2,1,0:T(8,128)} %get-tuple-element.10.t2, f32[24,128]{1,0:T(8,128)} %get-tuple-element.11.x2, ...), custom_call_target="tpu_custom_call" | custom-call | tf_op jit(solution)/shard_map/pallas_call | solution.py:540

commit v3 on v2

v3 whole, which is shorter than its diff:
```python
from functools import partial

import jax
import jax.numpy as jnp
import ml_dtypes
import numpy as np
from jax import lax
from jax.experimental import pallas as pl
from jax.experimental.pallas import tpu as pltpu
from jax.sharding import PartitionSpec as P

MESH = pl.DeviceIdType.MESH
F32 = jnp.float32
BF16 = jnp.bfloat16


def forms(level, n, last):
    step = 1 << level
    i = np.arange(n)

    def hat(i, index):
        value = np.maximum(0.0, 1.0 - np.abs(i - (step * index + step - 1)) / step)
        return np.where((i >= n) | (index >= n // step), 0.0, value) if last else value

    def slope(i, index):
        return hat(i, index) - hat(i + 1, index)

    def column(plus, index):
        other = index + plus
        return hat(i, index) * hat(i, other), slope(i, index) * slope(i, other)

    return column


def row_order(count):
    return (
        [(0, j) for j in range(count)]
        + [(1, j) for j in range(-1, count)]
        + [(0, -1), (0, count)]
    )


def y_rows(level, count):
    order = row_order(count)
    if level == 3:
        return dict(zip(order, range(len(order))))
    place = {(0, j): j for j in range(count)}
    place.update({(1, j): count + 8 + j for j in range(count)})
    place.update({(0, -1): count + 5, (0, count): count + 6, (1, -1): count + 7})
    return place


def weights_y(level, n, rows, last):
    column = forms(level, n, last)
    mass = np.zeros((rows, n))
    stiff = np.zeros((rows, n))
    for (plus, index), row in y_rows(level, n >> level).items():
        mass[row], stiff[row] = column(plus, index)
    first = np.concatenate([mass, mass, stiff, stiff], axis=1)
    second = np.concatenate([mass, mass], axis=1)
    return first, second


def lanes_of(level, n):
    count = n >> level
    if level == 3:
        return [(0, j) for j in range(-1, count + 1)] + [(1, j) for j in range(-1, count)], 128
    rim = 2 * count
    lanes = [(0, j) for j in range(count)] + [(1, j) for j in range(count)]
    lanes += [None] * (2 * count)
    lanes[rim] = (0, -1)
    lanes[rim + count // 2] = (0, count)
    lanes[rim + count] = (1, -1)
    return lanes, 4 * count


def weights_x(level, n, last):
    column = forms(level, n, last)
    lanes, width = lanes_of(level, n)
    mass = np.zeros((n, width))
    stiff = np.zeros((n, width))
    for lane, entry in enumerate(lanes):
        if entry is not None:
            mass[:, lane], stiff[:, lane] = column(*entry)
    scale = 0.5**level
    both = np.concatenate([mass, mass, stiff, stiff], axis=0) * scale
    return both


def place_x(blocks, count):
    whole = blocks * count
    out = np.zeros((blocks, 2, 128, 3 * 128))
    for block in range(blocks):
        for layer in range(3):
            entries = lanes_of(3, count * 8)[0]
            for lane, (plus, index) in enumerate(entries):
                source = 40 * layer + lane
                target = block * count + index
                if 0 <= target < whole:
                    out[block, :, source, layer * 128 + plus * whole + target] = 1.0
    return out.reshape(blocks * 256, 384).astype(ml_dtypes.bfloat16)


def place_y(blocks, count, rows, packed):
    whole = blocks * count
    out = np.zeros((rows, 2, blocks, packed))
    for block in range(blocks):
        for row, (plus, index) in enumerate(row_order(count)):
            target = block * count + index
            if 0 <= target < whole:
                out[target + plus * (whole + 8), :, block, row] = 1.0
    return out.reshape(rows, 2 * blocks * packed).astype(ml_dtypes.bfloat16)


def split(value):
    high = value.astype(BF16)
    return high, (value - high.astype(F32)).astype(BF16)


def dot(left, right):
    return jnp.dot(left, right, preferred_element_type=F32)


def roll(value, shift):
    return pltpu.roll(value, shift % 128, 1)


def mass_layers(field):
    n = len(field)
    quarter = [0.25 * field[2 * j] for j in range(n // 2)] + [None]
    same = {-1: quarter[0]}
    plus = {-1: quarter[0]}
    for j in range(n // 2):
        total = field[2 * j + 1] + quarter[j]
        same[j] = total if quarter[j + 1] is None else total + quarter[j + 1]
        plus[j] = quarter[j + 1]
    same[n // 2] = None
    return same, plus


def stiff_layers(field):
    n = len(field)
    share = {-1: 0.25 * field[0], n // 2 - 1: 0.25 * field[n - 1]}
    for j in range(n // 2 - 1):
        share[j] = 0.25 * (field[2 * j + 1] + field[2 * j + 2])
    same = {-1: share[-1], n // 2: share[n // 2 - 1]}
    for j in range(n // 2):
        same[j] = share[j - 1] + share[j]
    return same, share


def plus_of(a, b):
    if a is None:
        return b
    return a if b is None else a + b


def coarser(same, plus, count):
    def scaled(value, factor):
        return None if value is None else factor * value

    new_same, new_plus = {}, {}
    half = count // 2
    for j in range(-1, half + 1):
        total = scaled(plus_of(same.get(2 * j), same.get(2 * j + 2)), 0.25)
        for term in (same.get(2 * j + 1), plus.get(2 * j), plus.get(2 * j + 1)):
            total = plus_of(total, term)
        new_same[j] = total
    for j in range(-1, half):
        total = scaled(plus_of(plus.get(2 * j + 1), plus.get(2 * j + 2)), 0.5)
        new_plus[j] = plus_of(total, scaled(same.get(2 * j + 2), 0.25))
    return new_same, new_plus


def all_weights(last_x, last_y):
    x = np.zeros((512, 512))
    for level, start, width in ((1, 0, 256), (2, 256, 128), (3, 384, 128)):
        x[:, start:start + width] = weights_x(level, 128, last_x)
    y = np.zeros((64, 512))
    for level, row, rows, lane in ((1, 0, 48, 0), (2, 0, 32, 256), (3, 48, 16, 0)):
        first, second = weights_y(level, 32, rows, last_y)
        y[row:row + rows, lane:lane + 128] = first
        y[row:row + rows, lane + 128:lane + 192] = second
    return x.astype(ml_dtypes.bfloat16), y.astype(ml_dtypes.bfloat16)


S_PX, S_YD, S_YU, S_ROWS = 0, 64, 160, 216
R_X, R_YD, R_YU, R_D, R_ROWS = 0, 128, 224, 280, 344
Z_ONE, Z_SIDE, Z_TWO, Z_ROWS = 0, 40, 80, 104


def main_kernel(
    r_hbm, kz_hbm, ky_hbm, kx_hbm, wx_hbm, wy_hbm,
    t1, t2, own, rb, g3,
    f4, wx, wy, rims, rimr, zs, zr,
    ga1, gb1, ga2, gb2, ga3, gb3, c1, c2, c3, sb, p3,
    lsem, send, recv, gsend, grecv,
):
    gz, gy, gx = lax.axis_index("gz"), lax.axis_index("gy"), lax.axis_index("gx")
    nz, ny, nx = lax.axis_size("gz"), lax.axis_size("gy"), lax.axis_size("gx")
    zp, zm = lax.rem(gz + 1, nz), lax.rem(gz + nz - 1, nz)
    yp, ym = lax.rem(gy + 1, ny), lax.rem(gy + ny - 1, ny)
    xp, xm = lax.rem(gx + 1, nx), lax.rem(gx + nx - 1, nx)
    slab = ny * nx
    me = gy * nx + gx
    peers = []
    for d in range(1, slab):
        t = lax.rem(me + d, slab)
        peers.append((gz, lax.div(t, nx), lax.rem(t, nx)))

    barrier = pltpu.get_barrier_semaphore()
    others = [(zp, gy, gx), (zm, gy, gx)]
    for device in others + peers:
        pl.semaphore_signal(barrier, inc=1, device_id=device, device_id_type=MESH)

    end_x = jnp.where(gx == nx - 1, 1, 0)
    end_y = jnp.where(gy == ny - 1, 1, 0)
    loads = [
        pltpu.make_async_copy(f, f4.at[j], lsem.at[j])
        for j, f in enumerate((r_hbm, kz_hbm, ky_hbm, kx_hbm))
    ]
    loads.append(pltpu.make_async_copy(wx_hbm.at[end_x], wx, lsem.at[4]))
    loads.append(pltpu.make_async_copy(wy_hbm.at[end_y], wy, lsem.at[5]))
    for c in loads:
        c.start()

    started = []

    def copy(src, dst, device):
        k = len(started)
        c = pltpu.make_async_remote_copy(
            src_ref=src, dst_ref=dst, send_sem=send.at[k], recv_sem=recv.at[k],
            device_id=device, device_id_type=MESH,
        )
        c.start()
        started.append(c)
        return c

    for c in loads:
        c.wait()

    def layers(j):
        return [f4[j, k] for k in range(16)]

    same1, plus1 = mass_layers(layers(0))
    ssame, share = stiff_layers(layers(1))
    for j in range(-1, 9):
        same1[j] = plus_of(same1[j], ssame[j])
    for j in range(-1, 8):
        plus1[j] = -share[j] if plus1[j] is None else plus1[j] - share[j]
    level1 = [(same1, plus1), mass_layers(layers(2)), mass_layers(layers(3))]
    level2 = [coarser(*f, 8) for f in level1]
    level3 = [coarser(*f, 4) for f in level2]
    top_z, low_z = gz == nz - 1, gz == 0
    for level, n, factor in ((level1, 8, 3.0), (level2, 4, 15.0), (level3, 2, 63.0)):
        same, plus = level[0]
        last = jnp.where(top_z, same[n], 0.0)
        same[n - 1] = same[n - 1] + factor * last
        plus[n - 1] = plus[n - 1] + last

    zero = jnp.zeros((32, 128), F32)

    def put(ga, gb, j, values):
        lanes = pl.ds(128 * j, 128)
        for base, (ref, value) in enumerate(zip((ga, ga, gb), values)):
            high, low = split(zero if value is None else value)
            start = 64 * base if base < 2 else 0
            ref[start:start + 32, lanes] = high
            ref[start + 32:start + 64, lanes] = low

    def reduce_yx(level, count, ga, gb, wya, wyb, wxl, rows):
        order = row_order(count)
        for j, (plus, index) in enumerate(order):
            put(ga, gb, j, [f[plus][index] for f in level])
        left = []
        for value in (dot(wya, ga[...]), dot(wyb, gb[...])):
            stacked = jnp.concatenate(
                [value[:, 128 * j:128 * j + 128] for j in range(len(order))], axis=0
            )
            left += split(stacked)
        out = dot(jnp.concatenate(left, axis=1), wxl)
        return [out[rows * j:rows * j + rows] for j in range(len(order))]

    out3 = reduce_yx(
        level3, 2, ga3, gb3, wy[48:64, 0:128], wy[48:64, 128:192], wx[:, 384:512], 16
    )
    for k, j in enumerate((5, 2, 6)):
        rims[16 * k:16 * k + 16] = out3[j]
    for j in range(5):
        c3[j] = out3[j]
    pl.semaphore_wait(barrier, slab - 1 + len(others))
    round_z = [
        copy(rims.at[0:32], rimr.at[0:32], (zm, gy, gx)),
        copy(rims.at[32:48], rimr.at[32:48], (zp, gy, gx)),
    ]

    out2 = reduce_yx(
        level2, 4, ga2, gb2, wy[0:32, 256:384], wy[0:32, 384:448], wx[:, 256:384], 32
    )
    out2 = [value[0:24] for value in out2]
    out1 = reduce_yx(
        level1, 8, ga1, gb1, wy[0:48, 0:128], wy[0:48, 128:192], wx[:, 0:256], 48
    )
    side1 = [value[0:40, 128:256] for value in out1]
    out1 = [value[0:40, 0:128] for value in out1]
    for k, (one, two) in enumerate(((17, 9), (8, 4), (18, 10))):
        start = Z_ROWS * k
        zs[start + Z_ONE:start + Z_ONE + 40] = out1[one]
        zs[start + Z_SIDE:start + Z_SIDE + 40] = side1[one]
        zs[start + Z_TWO:start + Z_TWO + 24] = out2[two]
    faces = [
        copy(zs.at[pl.ds(0, 2 * Z_ROWS)], zr.at[pl.ds(0, 2 * Z_ROWS)], (zm, gy, gx)),
        copy(zs.at[pl.ds(2 * Z_ROWS, Z_ROWS)], zr.at[pl.ds(2 * Z_ROWS, Z_ROWS)], (zp, gy, gx)),
    ]

    lane2 = lax.broadcasted_iota(jnp.int32, (24, 128), 1)
    totals = [None, None]

    def pack(k, one, side, two):
        if one is not None:
            c1[k] = one
            totals[0] = plus_of(totals[0], roll(side, k) if k else side)
            for start, row in ((S_YD, 21), (S_YD + 40, 23), (S_YU + 16, 22)):
                sb[start + k:start + k + 1] = one[row:row + 1]
        if two is not None:
            c2[k] = two
            totals[1] = plus_of(
                totals[1], roll(jnp.where(lane2 >= 64, two, 0.0), 64 + k)
            )
            for start, row in ((S_YD, 13), (S_YD + 40, 15), (S_YU + 16, 14)):
                sb[start + 24 + k:start + 25 + k] = two[row:row + 1]

    blank = jnp.zeros((40, 128), F32)
    for start in (S_YD, S_YD + 40, S_YU + 16):
        sb[start:start + 40] = blank
    for k in range(17):
        if k not in (0, 7, 8, 16):
            pack(k, out1[k], side1[k], None)
    for k in range(9):
        if k not in (0, 3, 4, 8):
            pack(k, None, None, out2[k])

    for c in round_z:
        c.wait_recv()
    low = jnp.where(low_z, 0.0, rimr[32:48])
    fix3 = {
        0: low, 1: jnp.where(top_z, 0.0, rimr[0:16]),
        2: -low, 4: jnp.where(top_z, 0.0, rimr[16:32]),
    }
    packed = [None, None]
    for j in range(5):
        value = c3[j] if j not in fix3 else c3[j] + fix3[j]
        if j == 2:
            value = jnp.where(low_z, 0.0, value)
        packed[j // 3] = plus_of(packed[j // 3], roll(value, 40 * (j % 3)) if j % 3 else value)
    p3[0] = packed[0]
    p3[1] = packed[1]
    gather = []
    for d, device in enumerate(peers):
        c = pltpu.make_async_remote_copy(
            src_ref=p3, dst_ref=g3.at[me], send_sem=gsend.at[d], recv_sem=grecv.at[d],
            device_id=device, device_id_type=MESH,
        )
        c.start()
        gather.append(c)
    mine = pltpu.make_async_copy(p3, g3.at[me], lsem.at[3])
    mine.start()

    for c in faces:
        c.wait_recv()

    def came(k, start, rows):
        value = zr[Z_ROWS * k + start:Z_ROWS * k + start + rows]
        return jnp.where(low_z if k == 2 else top_z, 0.0, value)

    def fixed(values, n, start, rows):
        low = came(2, start, rows)
        return {
            0: values[0] + low,
            n - 1: values[n - 1] + came(0, start, rows),
            n: jnp.where(low_z, 0.0, values[n] - low),
            2 * n: values[2 * n] + came(1, start, rows),
        }

    one, side = fixed(out1, 8, Z_ONE, 40), fixed(side1, 8, Z_SIDE, 40)
    for k in one:
        pack(k, one[k], side[k], None)
    for k, value in fixed(out2, 4, Z_TWO, 24).items():
        pack(k, None, None, value)
    total1, total2 = totals
    sb[S_PX:S_PX + 16] = total1[0:16]
    sb[S_PX + 16:S_PX + 32] = total1[24:40]
    sb[S_PX + 32:S_PX + 40] = total2[0:8]
    sb[S_PX + 40:S_PX + 48] = total2[16:24]
    for start in (S_PX + 48, S_YD + 80, S_YU):
        sb[start:start + 8] = total1[16:24]
        sb[start + 8:start + 16] = total2[8:16]
    y_to, x_to = (ym, yp), (xm, xp)
    for yi in range(2):
        for xi in range(2):
            k = 16 * (2 * yi + xi)
            copy(
                sb.at[pl.ds(S_PX + 48, 16)], rb.at[pl.ds(R_D + k, 16)], (gz, y_to[yi], x_to[xi])
            )
    for k in range(2):
        copy(sb.at[pl.ds(S_PX, 64)], rb.at[pl.ds(R_X + 64 * k, 64)], (gz, gy, x_to[k]))
    copy(sb.at[pl.ds(S_YD, 96)], rb.at[pl.ds(R_YD, 96)], (gz, ym, gx))
    copy(sb.at[pl.ds(S_YU, 56)], rb.at[pl.ds(R_YU, 56)], (gz, yp, gx))

    stores = [
        pltpu.make_async_copy(c1, t1, lsem.at[0]),
        pltpu.make_async_copy(c2, t2, lsem.at[1]),
        pltpu.make_async_copy(sb.at[pl.ds(S_PX, 64)], own, lsem.at[2]),
    ]
    for c in stores:
        c.start()
    for c in stores:
        c.wait()
    mine.wait()
    for c in started[4:]:
        c.wait_recv()
    for c in gather:
        c.wait()
    for c in started:
        c.wait_send()


def finish_kernel(
    t1_hbm, t2_hbm, own_hbm, rb_hbm, g3_hbm, qx_hbm, qy_hbm, o1, o2, o3,
    t1, t2, px, rb, g3, qx, qy, x1, x2, q3, s3, v1, v2, v3, csem, osem,
):
    gy, gx = lax.axis_index("gy"), lax.axis_index("gx")
    ny, nx = lax.axis_size("gy"), lax.axis_size("gx")
    loads = [
        pltpu.make_async_copy(src, dst, csem.at[k])
        for k, (src, dst) in enumerate((
            (rb_hbm, rb), (t1_hbm, t1), (t2_hbm, t2), (own_hbm, px.at[0]),
            (g3_hbm, g3), (qx_hbm, qx), (qy_hbm, qy),
        ))
    ]
    for c in loads:
        c.start()

    def present(flag):
        return jnp.where(flag, 1.0, 0.0).astype(F32)

    from_up_y, from_low_y = present(gy < ny - 1), present(gy > 0)
    from_up_x, from_low_x = present(gx < nx - 1), present(gx > 0)
    for c in loads[0:4]:
        c.wait()

    for k in range(2):
        px[1 + k] = rb[R_X + 64 * k:R_X + 64 * k + 64]
    side = [(rb[R_YD + 80:R_YD + 96], rb[R_YU:R_YU + 16])]
    for xi in range(2):
        side.append(tuple(rb[R_D + 16 * k:R_D + 16 * k + 16] for k in (xi, 2 + xi)))
    for k, (upper, lower) in enumerate(side):
        upper, lower = from_up_y * upper, from_low_y * lower
        for same, plus, rim, group in ((0, 16, 48, 0), (32, 40, 56, 8)):
            n = plus - same
            for row, value in (
                (same + n - 1, upper[group + 5:group + 6]),
                (plus + n - 1, upper[group + 7:group + 8]),
                (same, lower[group + 6:group + 7]),
            ):
                px[k, row:row + 1] = px[k, row:row + 1] + value
            row = rim + 7
            px[k, row:row + 1] = (px[k, row:row + 1] - lower[group + 6:group + 7]) * from_low_y

    sets = (
        (t1, x1, 8, 16, 64, (0, 16, 48), 0),
        (t2, x2, 4, 8, 32, (32, 40, 56), 24),
    )
    for t, x, lz, n, lanes, parts, rows_at in sets:
        count = 2 * lz + 1
        size = 24 if n == 16 else 16
        same_up = from_up_y * rb[R_YD + rows_at:R_YD + rows_at + size]
        plus_up = from_up_y * rb[R_YD + 40 + rows_at:R_YD + 40 + rows_at + size]
        low = from_low_y * rb[R_YU + 16 + rows_at:R_YU + 16 + rows_at + size]
        for j in range(count):
            t[j, n - 1:n] = t[j, n - 1:n] + same_up[j:j + 1]
            t[j, 2 * n + 7:2 * n + 8] = t[j, 2 * n + 7:2 * n + 8] + plus_up[j:j + 1]
            t[j, 0:1] = t[j, 0:1] + low[j:j + 1]
            t[j, n + 7:n + 8] = (t[j, n + 7:n + 8] - low[j:j + 1]) * from_low_y

        def column(k):
            same, plus, rim = (px[k, s:s + z] for s, z in zip(parts, (n, n, 8)))
            return jnp.concatenate([same, rim, plus], axis=0)

        above, below = from_up_x * column(1), from_low_x * column(2)
        x[...] = (column(0) - roll(below, lanes // 2)) * from_low_x
        lane = lax.broadcasted_iota(jnp.int32, above.shape, 1)
        at_end = (lane == lanes - 1) | (lane == 2 * lanes - 1)
        for j in range(count):
            value = t[j] + jnp.where(at_end, roll(above, lanes - 1 - j), 0.0)
            t[j] = value + jnp.where(lane == 0, roll(below, -(lanes // 2) - j), 0.0)

    pending = []

    def expand(t, x, v, o, nz, ny, n):
        done = [set() for _ in range(3)]
        rows = {0: slice(ny + 7, 2 * ny + 7), 1: slice(0, ny), 2: slice(ny + 8, 2 * ny + 8)}
        for k in range(2 * nz + 1):
            value = t[k]
            first = 0.0 if x is None else roll(x[...], -(n + k))
            lane = lax.broadcasted_iota(jnp.int32, value.shape, 1)
            low = jnp.where(lane == 0, first, roll(value, 1 - n))
            planes = (low, value, roll(value, -n))
            if k < nz:
                targets = [(1, k)]
            else:
                targets = [(0, k - nz)] if k - nz < nz else []
                targets += [(2, k - nz - 1)] if k > nz else []
            for c, plane in enumerate(planes):
                plane = plane[:, 0:n]
                for a, layer in targets:
                    for b in range(3):
                        v[9 * a + 3 * b + c, layer] = plane[rows[b]]
            for a, layer in targets:
                done[a].add(layer)
                if len(done[a]) == nz:
                    part = pl.ds(9 * a, 9)
                    copy = pltpu.make_async_copy(v.at[part], o.at[part], osem.at[len(pending)])
                    copy.start()
                    pending.append(copy)

    expand(t1, x1, v1, o1, 8, 16, 64)
    expand(t2, x2, v2, o2, 4, 8, 32)

    for c in loads[4:]:
        c.wait()
    left = []
    for bx in range(4):
        blocks = [g3[4 * by + bx].reshape(32, 128) for by in range(4)]
        left += split(jnp.concatenate(blocks, axis=0))
    q3[...] = dot(jnp.concatenate(left, axis=1), qx[...])
    for h in range(2):
        rows = jnp.concatenate(
            [q3[32 * by + 16 * h:32 * by + 16 * h + 16, :] for by in range(4)], axis=0
        )
        placed = dot(qy[...], jnp.concatenate(split(rows), axis=0))
        for j in range(3):
            if 3 * h + j < 5:
                s3[3 * h + j] = placed[0:40, 128 * j:128 * j + 128]
    expand(s3, None, v3, o3, 2, 16, 64)
    for copy in pending:
        copy.wait()


def shards(coeff_z, coeff_y, coeff_x, reaction):
    hbm = pl.BlockSpec(memory_space=pltpu.HBM)
    shape = jax.ShapeDtypeStruct
    v = pltpu.VMEM
    dma = pltpu.SemaphoreType.DMA
    pairs = [all_weights(flag, flag) for flag in (False, True)]
    wx, wy = (jnp.asarray(np.stack([pair[k] for pair in pairs])) for k in range(2))
    between = (
        shape((17, 40, 128), F32), shape((9, 24, 128), F32), shape((64, 128), F32),
        shape((R_ROWS, 128), F32), shape((16, 2, 16, 128), F32),
    )
    middle = pl.pallas_call(
        main_kernel,
        out_shape=between,
        in_specs=[hbm] * 6,
        out_specs=(hbm,) * 5,
        scratch_shapes=[
            v((4, 16, 32, 128), F32), v((512, 512), BF16), v((64, 512), BF16),
            v((48, 128), F32), v((48, 128), F32),
            v((3 * Z_ROWS, 128), F32), v((3 * Z_ROWS, 128), F32),
            v((128, 19 * 128), BF16), v((64, 19 * 128), BF16),
            v((128, 11 * 128), BF16), v((64, 11 * 128), BF16),
            v((128, 7 * 128), BF16), v((64, 7 * 128), BF16),
            v((17, 40, 128), F32), v((9, 24, 128), F32), v((5, 16, 128), F32),
            v((S_ROWS, 128), F32), v((2, 16, 128), F32),
            dma((6,)), dma((12,)), dma((12,)), dma((15,)), dma((15,)),
        ],
        compiler_params=pltpu.CompilerParams(
            collective_id=0, has_side_effects=True, vmem_limit_bytes=62 << 20
        ),
    )(reaction, coeff_z, coeff_y, coeff_x, wx, wy)
    return pl.pallas_call(
        finish_kernel,
        out_shape=(
            shape((27, 8, 16, 64), F32), shape((27, 4, 8, 32), F32), shape((27, 2, 16, 64), F32),
        ),
        in_specs=[hbm] * 7,
        out_specs=(hbm,) * 3,
        scratch_shapes=[
            v((17, 40, 128), F32), v((9, 24, 128), F32), v((3, 64, 128), F32),
            v((R_ROWS, 128), F32), v((16, 2, 16, 128), F32),
            v((1024, 384), BF16), v((48, 128), BF16), v((40, 128), F32), v((24, 128), F32),
            v((128, 384), F32), v((5, 40, 128), F32),
            v((27, 8, 16, 64), F32), v((27, 4, 8, 32), F32), v((27, 2, 16, 64), F32),
            dma((7,)), dma((9,)),
        ],
        compiler_params=pltpu.CompilerParams(vmem_limit_bytes=62 << 20),
    )(*middle, jnp.asarray(place_x(4, 16)), jnp.asarray(place_y(4, 4, 48, 16)))


def solution(mesh):
    in_specs = (P("gz", "gy", "gx"),) * 4
    out_specs = (P(None, "gz", "gy", "gx"), P(None, "gz", "gy", "gx"), P(None, "gz", None, None))
    return jax.shard_map(shards, mesh=mesh, in_specs=in_specs, out_specs=out_specs, check_vma=False)
```

time: 25.5 us -> 23.3 us (0.914)
  Pallas kernels: 24.7 us -> 22.5 us
    pallas_call x2, Pallas kernels: 24.7 us -> 22.5 us  [the longest x1 19.3 us: shards(): pl.pallas_call(main_kernel, out_shape=between, in_specs=[hbm] * 6, out_sp...]
where the time goes in v3:
time: 23.3 us; the launch traced here: 23.2 us
  Pallas kernels  22.5 us (97%)
  between operations  0.64 us (3%)
    pallas_call x1, Pallas kernels, shards(): pl.pallas_call(main_kernel, out_shape=between, in_specs=[hbm] * 6, out_sp...  19.3 us
    pallas_call x1, Pallas kernels, shards(): pl.pallas_call(finish_kernel, out_shape=(shape((27, 8, 16, 64), F32), sha...  3.23 us

profile of v3, /device:TPU:1, one launch (start us, length us, event | category | flops | bytes accessed | tf_op | source)
XLA Modules:
  0.0 23.2 jit_solution(3117192139351338428)
XLA Ops:
  0.6 19.3 %shard_map.103 = (f32[17,40,128]{2,1,0:T(8,128)}, f32[9,24,128]{2,1,0:T(8,128)}, f32[64,128]{1,0:T(8,128)}, f32[344,128]{1,0:T(8,128)}, f32[16,2,16,128]{3,2,1,0:T(8,128)}) custom-call(f32[16,32,128]{2,1,0:T(8,128)} %r_hbm.1, f32[16,32,128]{2,1,0:T(8,128)} %kz_hbm.1, f32[16,32,128]{2,1,0:T(8,128)} %ky_hbm.1, f32[16,32,128]{2,1,0:T(8,128)} %kx_hbm.1, ...), custom_call_target="tpu_custom_call" | custom-call | tf_op jit(solution)/shard_map/pallas_call | solution.py:561
  19.9 3.2 %shard_map.104 = (f32[27,8,16,64]{3,2,1,0:T(8,128)}, f32[27,4,8,32]{3,2,1,0:T(8,128)}, f32[27,2,16,64]{3,2,1,0:T(8,128)}) custom-call(f32[17,40,128]{2,1,0:T(8,128)} %get-tuple-element.8.t1_hbm, f32[9,24,128]{2,1,0:T(8,128)} %get-tuple-element.9.t2_hbm, f32[64,128]{1,0:T(8,128)} %get-tuple-element.10.own_hbm, f32[344,128]{1,0:T(8,128)} %get-tuple-element.11.rb_hbm, ...), custom_call_target="tpu_custom_call" | custom-call | tf_op jit(solution)/shard_map/pallas_call | solution.py:581

commit v4 on v3

--- a/solution.py
+++ b/solution.py
@@ -87,28 +87,22 @@
     return both
 
 
-def place_x(blocks, count):
-    whole = blocks * count
-    out = np.zeros((blocks, 2, 128, 3 * 128))
-    for block in range(blocks):
-        for layer in range(3):
-            entries = lanes_of(3, count * 8)[0]
-            for lane, (plus, index) in enumerate(entries):
-                source = 40 * layer + lane
-                target = block * count + index
-                if 0 <= target < whole:
-                    out[block, :, source, layer * 128 + plus * whole + target] = 1.0
-    return out.reshape(blocks * 256, 384).astype(ml_dtypes.bfloat16)
-
-
-def place_y(blocks, count, rows, packed):
+def place_x(count):
+    out = np.zeros((2, 128, 3 * 128))
+    for layer in range(3):
+        for lane, (plus, index) in enumerate(lanes_of(3, count * 8)[0]):
+            out[:, 40 * layer + lane, layer * 128 + plus * 64 + count + index] = 1.0
+    return out.reshape(256, 384).astype(ml_dtypes.bfloat16)
+
+
+def place_y(blocks, count, rows, packed, shift):
     whole = blocks * count
     out = np.zeros((rows, 2, blocks, packed))
     for block in range(blocks):
         for row, (plus, index) in enumerate(row_order(count)):
             target = block * count + index
             if 0 <= target < whole:
-                out[target + plus * (whole + 8), :, block, row] = 1.0
+                out[target + plus * (whole + 8), :, block, row + shift] = 1.0
     return out.reshape(rows, 2 * blocks * packed).astype(ml_dtypes.bfloat16)
 
 
@@ -184,16 +178,16 @@
     return x.astype(ml_dtypes.bfloat16), y.astype(ml_dtypes.bfloat16)
 
 
-S_PX, S_YD, S_YU, S_ROWS = 0, 64, 160, 216
-R_X, R_YD, R_YU, R_D, R_ROWS = 0, 128, 224, 280, 344
-Z_ONE, Z_SIDE, Z_TWO, Z_ROWS = 0, 40, 80, 104
+S_PX, S_YD, S_YU, S_ROWS = 0, 64, 144, 192
+R_X, R_YD, R_YU, R_D, R_ROWS = 0, 128, 208, 256, 320
+Z_ONE, Z_TWO, Z_THREE, Z_ROWS = 0, 40, 64, 80
 
 
 def main_kernel(
     r_hbm, kz_hbm, ky_hbm, kx_hbm, wx_hbm, wy_hbm,
     t1, t2, own, rb, g3,
-    f4, wx, wy, rims, rimr, zs, zr,
-    ga1, gb1, ga2, gb2, ga3, gb3, c1, c2, c3, sb, p3,
+    f4, wx, wy, zs, zr,
+    gaf, gbf, ga1, gb1, ga2, gb2, ga3, gb3, c1, c2, c3, sb, p3,
     lsem, send, recv, gsend, grecv,
 ):
     gz, gy, gx = lax.axis_index("gz"), lax.axis_index("gy"), lax.axis_index("gx")
@@ -203,10 +197,8 @@
     xp, xm = lax.rem(gx + 1, nx), lax.rem(gx + nx - 1, nx)
     slab = ny * nx
     me = gy * nx + gx
-    peers = []
-    for d in range(1, slab):
-        t = lax.rem(me + d, slab)
-        peers.append((gz, lax.div(t, nx), lax.rem(t, nx)))
+    offsets = [(dy, dx) for dx in (2, 1, 3, 0) for dy in (2, 1, 3, 0) if dy or dx]
+    peers = [(gz, lax.rem(gy + dy, ny), lax.rem(gx + dx, nx)) for dy, dx in offsets]
 
     barrier = pltpu.get_barrier_semaphore()
     others = [(zp, gy, gx), (zm, gy, gx)]
@@ -268,50 +260,54 @@
             ref[start:start + 32, lanes] = high
             ref[start + 32:start + 64, lanes] = low
 
-    def reduce_yx(level, count, ga, gb, wya, wyb, wxl, rows):
+    def reduce_yx(level, count, places, ga, gb, wya, wyb, wxl, rows):
         order = row_order(count)
-        for j, (plus, index) in enumerate(order):
+        for j, k in enumerate(places):
+            plus, index = order[k]
             put(ga, gb, j, [f[plus][index] for f in level])
+        size = len(places)
         left = []
-        for value in (dot(wya, ga[...]), dot(wyb, gb[...])):
+        for value in (dot(wya, ga[:, 0:128 * size]), dot(wyb, gb[:, 0:128 * size])):
             stacked = jnp.concatenate(
-                [value[:, 128 * j:128 * j + 128] for j in range(len(order))], axis=0
+                [value[:, 128 * j:128 * j + 128] for j in range(size)], axis=0
             )
             left += split(stacked)
         out = dot(jnp.concatenate(left, axis=1), wxl)
-        return [out[rows * j:rows * j + rows] for j in range(len(order))]
+        return {k: out[rows * j:rows * j + rows] for j, k in enumerate(places)}
+
+    def reduce_one(places, ga, gb):
+        out = reduce_yx(
+            level1, 8, places, ga, gb, wy[0:48, 0:128], wy[0:48, 128:192], wx[:, 0:256], 48
+        )
+        for k, value in out.items():
+            side1[k] = value[0:40, 128:256]
+            out1[k] = value[0:40, 0:128]
 
     out3 = reduce_yx(
-        level3, 2, ga3, gb3, wy[48:64, 0:128], wy[48:64, 128:192], wx[:, 384:512], 16
+        level3, 2, range(7), ga3, gb3, wy[48:64, 0:128], wy[48:64, 128:192], wx[:, 384:512], 16
     )
-    for k, j in enumerate((5, 2, 6)):
-        rims[16 * k:16 * k + 16] = out3[j]
+    out2 = reduce_yx(
+        level2, 4, range(11), ga2, gb2, wy[0:32, 256:384], wy[0:32, 384:448], wx[:, 256:384], 32
+    )
+    out2 = {k: value[0:24] for k, value in out2.items()}
+    out1, side1 = {}, {}
+    reduce_one((8, 17, 18), gaf, gbf)
+    lane1 = lax.broadcasted_iota(jnp.int32, (40, 128), 1)
+    low_pair, high_one = (lane1 == 65) | (lane1 == 97), lane1 == 69
+    for k, (one, two, three) in enumerate(((17, 9, 5), (8, 4, 2), (18, 10, 6))):
+        start = Z_ROWS * k
+        zs[start + Z_ONE:start + Z_ONE + 40] = out1[one]
+        rest = jnp.concatenate([out2[two], out3[three]], axis=0)
+        rest = jnp.where(low_pair, roll(side1[one], 65), rest)
+        zs[start + Z_TWO:start + Z_ROWS] = jnp.where(high_one, roll(side1[one], 5), rest)
     for j in range(5):
         c3[j] = out3[j]
     pl.semaphore_wait(barrier, slab - 1 + len(others))
-    round_z = [
-        copy(rims.at[0:32], rimr.at[0:32], (zm, gy, gx)),
-        copy(rims.at[32:48], rimr.at[32:48], (zp, gy, gx)),
-    ]
-
-    out2 = reduce_yx(
-        level2, 4, ga2, gb2, wy[0:32, 256:384], wy[0:32, 384:448], wx[:, 256:384], 32
-    )
-    out2 = [value[0:24] for value in out2]
-    out1 = reduce_yx(
-        level1, 8, ga1, gb1, wy[0:48, 0:128], wy[0:48, 128:192], wx[:, 0:256], 48
-    )
-    side1 = [value[0:40, 128:256] for value in out1]
-    out1 = [value[0:40, 0:128] for value in out1]
-    for k, (one, two) in enumerate(((17, 9), (8, 4), (18, 10))):
-        start = Z_ROWS * k
-        zs[start + Z_ONE:start + Z_ONE + 40] = out1[one]
-        zs[start + Z_SIDE:start + Z_SIDE + 40] = side1[one]
-        zs[start + Z_TWO:start + Z_TWO + 24] = out2[two]
     faces = [
         copy(zs.at[pl.ds(0, 2 * Z_ROWS)], zr.at[pl.ds(0, 2 * Z_ROWS)], (zm, gy, gx)),
         copy(zs.at[pl.ds(2 * Z_ROWS, Z_ROWS)], zr.at[pl.ds(2 * Z_ROWS, Z_ROWS)], (zp, gy, gx)),
     ]
+    reduce_one(tuple(range(8)) + tuple(range(9, 17)), ga1, gb1)
 
     lane2 = lax.broadcasted_iota(jnp.int32, (24, 128), 1)
     totals = [None, None]
@@ -320,19 +316,19 @@
         if one is not None:
             c1[k] = one
             totals[0] = plus_of(totals[0], roll(side, k) if k else side)
-            for start, row in ((S_YD, 21), (S_YD + 40, 23), (S_YU + 16, 22)):
+            for start, row in ((S_YD, 21), (S_YD + 32, 23), (S_YU + 16, 22)):
                 sb[start + k:start + k + 1] = one[row:row + 1]
         if two is not None:
             c2[k] = two
             totals[1] = plus_of(
                 totals[1], roll(jnp.where(lane2 >= 64, two, 0.0), 64 + k)
             )
-            for start, row in ((S_YD, 13), (S_YD + 40, 15), (S_YU + 16, 14)):
-                sb[start + 24 + k:start + 25 + k] = two[row:row + 1]
-
-    blank = jnp.zeros((40, 128), F32)
-    for start in (S_YD, S_YD + 40, S_YU + 16):
-        sb[start:start + 40] = blank
+            for start, row in ((S_YD, 13), (S_YD + 32, 15), (S_YU + 16, 14)):
+                sb[start + 17 + k:start + 18 + k] = two[row:row + 1]
+
+    blank = jnp.zeros((32, 128), F32)
+    for start in (S_YD, S_YD + 32, S_YU + 16):
+        sb[start:start + 32] = blank
     for k in range(17):
         if k not in (0, 7, 8, 16):
             pack(k, out1[k], side1[k], None)
@@ -340,21 +336,24 @@
         if k not in (0, 3, 4, 8):
             pack(k, None, None, out2[k])
 
-    for c in round_z:
+    for c in faces:
         c.wait_recv()
-    low = jnp.where(low_z, 0.0, rimr[32:48])
-    fix3 = {
-        0: low, 1: jnp.where(top_z, 0.0, rimr[0:16]),
-        2: -low, 4: jnp.where(top_z, 0.0, rimr[16:32]),
-    }
+
+    def came(k, start, rows):
+        value = zr[Z_ROWS * k + start:Z_ROWS * k + start + rows]
+        return jnp.where(low_z if k == 2 else top_z, 0.0, value)
+
+    lane3 = lax.broadcasted_iota(jnp.int32, (16, 128), 1)
+    down0, down1, low = (jnp.where(lane3 < 40, came(k, Z_THREE, 16), 0.0) for k in range(3))
+    fix3 = {0: low, 1: down0, 2: -low, 4: down1}
     packed = [None, None]
     for j in range(5):
         value = c3[j] if j not in fix3 else c3[j] + fix3[j]
         if j == 2:
             value = jnp.where(low_z, 0.0, value)
         packed[j // 3] = plus_of(packed[j // 3], roll(value, 40 * (j % 3)) if j % 3 else value)
-    p3[0] = packed[0]
-    p3[1] = packed[1]
+    p3[0:16] = packed[0]
+    p3[12:24] = packed[1][0:12]
     gather = []
     for d, device in enumerate(peers):
         c = pltpu.make_async_remote_copy(
@@ -366,33 +365,34 @@
     mine = pltpu.make_async_copy(p3, g3.at[me], lsem.at[3])
     mine.start()
 
-    for c in faces:
-        c.wait_recv()
-
-    def came(k, start, rows):
-        value = zr[Z_ROWS * k + start:Z_ROWS * k + start + rows]
-        return jnp.where(low_z if k == 2 else top_z, 0.0, value)
-
-    def fixed(values, n, start, rows):
-        low = came(2, start, rows)
+    def came_side(k):
+        value = came(k, Z_TWO, 40)
+        return roll(jnp.where(low_pair, value, 0.0), -65) + roll(jnp.where(high_one, value, 0.0), -5)
+
+    def came_two(k):
+        value = came(k, Z_TWO, 24)
+        return jnp.where((lane2 == 65) | (lane2 == 97) | (lane2 == 69), 0.0, value)
+
+    def fixed(values, n, part):
+        low = part(2)
         return {
             0: values[0] + low,
-            n - 1: values[n - 1] + came(0, start, rows),
+            n - 1: values[n - 1] + part(0),
             n: jnp.where(low_z, 0.0, values[n] - low),
-            2 * n: values[2 * n] + came(1, start, rows),
+            2 * n: values[2 * n] + part(1),
         }
 
-    one, side = fixed(out1, 8, Z_ONE, 40), fixed(side1, 8, Z_SIDE, 40)
+    one, side = fixed(out1, 8, lambda k: came(k, Z_ONE, 40)), fixed(side1, 8, came_side)
     for k in one:
         pack(k, one[k], side[k], None)
-    for k, value in fixed(out2, 4, Z_TWO, 24).items():
+    for k, value in fixed(out2, 4, came_two).items():
         pack(k, None, None, value)
     total1, total2 = totals
     sb[S_PX:S_PX + 16] = total1[0:16]
     sb[S_PX + 16:S_PX + 32] = total1[24:40]
     sb[S_PX + 32:S_PX + 40] = total2[0:8]
     sb[S_PX + 40:S_PX + 48] = total2[16:24]
-    for start in (S_PX + 48, S_YD + 80, S_YU):
+    for start in (S_PX + 48, S_YD + 64, S_YU):
         sb[start:start + 8] = total1[16:24]
         sb[start + 8:start + 16] = total2[8:16]
     y_to, x_to = (ym, yp), (xm, xp)
@@ -404,8 +404,8 @@
             )
     for k in range(2):
         copy(sb.at[pl.ds(S_PX, 64)], rb.at[pl.ds(R_X + 64 * k, 64)], (gz, gy, x_to[k]))
-    copy(sb.at[pl.ds(S_YD, 96)], rb.at[pl.ds(R_YD, 96)], (gz, ym, gx))
-    copy(sb.at[pl.ds(S_YU, 56)], rb.at[pl.ds(R_YU, 56)], (gz, yp, gx))
+    copy(sb.at[pl.ds(S_YD, 80)], rb.at[pl.ds(R_YD, 80)], (gz, ym, gx))
+    copy(sb.at[pl.ds(S_YU, 48)], rb.at[pl.ds(R_YU, 48)], (gz, yp, gx))
 
     stores = [
         pltpu.make_async_copy(c1, t1, lsem.at[0]),
@@ -417,7 +417,7 @@
     for c in stores:
         c.wait()
     mine.wait()
-    for c in started[4:]:
+    for c in started[2:]:
         c.wait_recv()
     for c in gather:
         c.wait()
@@ -451,7 +451,7 @@
 
     for k in range(2):
         px[1 + k] = rb[R_X + 64 * k:R_X + 64 * k + 64]
-    side = [(rb[R_YD + 80:R_YD + 96], rb[R_YU:R_YU + 16])]
+    side = [(rb[R_YD + 64:R_YD + 80], rb[R_YU:R_YU + 16])]
     for xi in range(2):
         side.append(tuple(rb[R_D + 16 * k:R_D + 16 * k + 16] for k in (xi, 2 + xi)))
     for k, (upper, lower) in enumerate(side):
@@ -469,14 +469,13 @@
 
     sets = (
         (t1, x1, 8, 16, 64, (0, 16, 48), 0),
-        (t2, x2, 4, 8, 32, (32, 40, 56), 24),
+        (t2, x2, 4, 8, 32, (32, 40, 56), 17),
     )
     for t, x, lz, n, lanes, parts, rows_at in sets:
         count = 2 * lz + 1
-        size = 24 if n == 16 else 16
-        same_up = from_up_y * rb[R_YD + rows_at:R_YD + rows_at + size]
-        plus_up = from_up_y * rb[R_YD + 40 + rows_at:R_YD + 40 + rows_at + size]
-        low = from_low_y * rb[R_YU + 16 + rows_at:R_YU + 16 + rows_at + size]
+        same_up = from_up_y * rb[R_YD + rows_at:R_YD + rows_at + count]
+        plus_up = from_up_y * rb[R_YD + 32 + rows_at:R_YD + 32 + rows_at + count]
+        low = from_low_y * rb[R_YU + 16 + rows_at:R_YU + 16 + rows_at + count]
         for j in range(count):
             t[j, n - 1:n] = t[j, n - 1:n] + same_up[j:j + 1]
             t[j, 2 * n + 7:2 * n + 8] = t[j, 2 * n + 7:2 * n + 8] + plus_up[j:j + 1]
@@ -529,16 +528,26 @@
 
     for c in loads[4:]:
         c.wait()
-    left = []
-    for bx in range(4):
-        blocks = [g3[4 * by + bx].reshape(32, 128) for by in range(4)]
-        left += split(jnp.concatenate(blocks, axis=0))
-    q3[...] = dot(jnp.concatenate(left, axis=1), qx[...])
+    blocks = jnp.concatenate(split(g3[...].reshape(384, 128)), axis=1)
+    spread = dot(blocks, qx[...])
+    lane = lax.broadcasted_iota(jnp.int32, (24, 128), 1)
+    for by in range(4):
+        for layer in range(3):
+            total = None
+            for bx in range(4):
+                at = 24 * (4 * by + bx)
+                part = spread[at:at + 24, 128 * layer:128 * layer + 128]
+                if bx != 1:
+                    part = roll(part, 16 * (bx - 1))
+                if bx == 0:
+                    part = jnp.where((lane == 63) | (lane == 127), 0.0, part)
+                total = plus_of(total, part)
+            q3[24 * by:24 * by + 24, 128 * layer:128 * layer + 128] = total
     for h in range(2):
         rows = jnp.concatenate(
-            [q3[32 * by + 16 * h:32 * by + 16 * h + 16, :] for by in range(4)], axis=0
+            [q3[24 * by + 8 * h:24 * by + 8 * h + 16, :] for by in range(4)], axis=0
         )
-        placed = dot(qy[...], jnp.concatenate(split(rows), axis=0))
+        placed = dot(qy[h], jnp.concatenate(split(rows), axis=0))
         for j in range(3):
             if 3 * h + j < 5:
                 s3[3 * h + j] = placed[0:40, 128 * j:128 * j + 128]
@@ -556,8 +565,9 @@
     wx, wy = (jnp.asarray(np.stack([pair[k] for pair in pairs])) for k in range(2))
     between = (
         shape((17, 40, 128), F32), shape((9, 24, 128), F32), shape((64, 128), F32),
-        shape((R_ROWS, 128), F32), shape((16, 2, 16, 128), F32),
+        shape((R_ROWS, 128), F32), shape((16, 24, 128), F32),
     )
+    place = jnp.asarray(np.stack([place_y(4, 4, 48, 16, shift) for shift in (0, 4)]))
     middle = pl.pallas_call(
         main_kernel,
         out_shape=between,
@@ -565,14 +575,14 @@
         out_specs=(hbm,) * 5,
         scratch_shapes=[
             v((4, 16, 32, 128), F32), v((512, 512), BF16), v((64, 512), BF16),
-            v((48, 128), F32), v((48, 128), F32),
             v((3 * Z_ROWS, 128), F32), v((3 * Z_ROWS, 128), F32),
-            v((128, 19 * 128), BF16), v((64, 19 * 128), BF16),
+            v((128, 3 * 128), BF16), v((64, 3 * 128), BF16),
+            v((128, 16 * 128), BF16), v((64, 16 * 128), BF16),
             v((128, 11 * 128), BF16), v((64, 11 * 128), BF16),
             v((128, 7 * 128), BF16), v((64, 7 * 128), BF16),
             v((17, 40, 128), F32), v((9, 24, 128), F32), v((5, 16, 128), F32),
-            v((S_ROWS, 128), F32), v((2, 16, 128), F32),
-            dma((6,)), dma((12,)), dma((12,)), dma((15,)), dma((15,)),
+            v((S_ROWS, 128), F32), v((24, 128), F32),
+            dma((6,)), dma((10,)), dma((10,)), dma((15,)), dma((15,)),
         ],
         compiler_params=pltpu.CompilerParams(
             collective_id=0, has_side_effects=True, vmem_limit_bytes=62 << 20
@@ -587,14 +597,14 @@
         out_specs=(hbm,) * 3,
         scratch_shapes=[
             v((17, 40, 128), F32), v((9, 24, 128), F32), v((3, 64, 128), F32),
-            v((R_ROWS, 128), F32), v((16, 2, 16, 128), F32),
-            v((1024, 384), BF16), v((48, 128), BF16), v((40, 128), F32), v((24, 128), F32),
-            v((128, 384), F32), v((5, 40, 128), F32),
+            v((R_ROWS, 128), F32), v((16, 24, 128), F32),
+            v((256, 384), BF16), v((2, 48, 128), BF16), v((40, 128), F32), v((24, 128), F32),
+            v((96, 384), F32), v((5, 40, 128), F32),
             v((27, 8, 16, 64), F32), v((27, 4, 8, 32), F32), v((27, 2, 16, 64), F32),
             dma((7,)), dma((9,)),
         ],
         compiler_params=pltpu.CompilerParams(vmem_limit_bytes=62 << 20),
-    )(*middle, jnp.asarray(place_x(4, 16)), jnp.asarray(place_y(4, 4, 48, 16)))
+    )(*middle, jnp.asarray(place_x(16)), place)
 
 
 def solution(mesh):

time: 23.3 us -> 22.3 us (0.957)
  Pallas kernels: 22.5 us -> 21.5 us
    pallas_call x1, Pallas kernels: 19.3 us -> 18.2 us  [shards(): pl.pallas_call(main_kernel, out_shape=between, in_specs=[hbm] * 6, out_sp...]
where the time goes in v4:
time: 22.3 us; the launch traced here: 22.2 us
  Pallas kernels  21.5 us (96%)
  between operations  0.64 us (3%)
    pallas_call x1, Pallas kernels, shards(): pl.pallas_call(main_kernel, out_shape=between, in_specs=[hbm] * 6, out_sp...  18.2 us
    pallas_call x1, Pallas kernels, shards(): pl.pallas_call(finish_kernel, out_shape=(shape((27, 8, 16, 64), F32), sha...  3.28 us

profile of v4, /device:TPU:1, one launch (start us, length us, event | category | flops | bytes accessed | tf_op | source)
XLA Modules:
  0.0 22.2 jit_solution(17883479402106791429)
XLA Ops:
  0.6 18.2 %shard_map.103 = (f32[17,40,128]{2,1,0:T(8,128)}, f32[9,24,128]{2,1,0:T(8,128)}, f32[64,128]{1,0:T(8,128)}, f32[320,128]{1,0:T(8,128)}, f32[16,24,128]{2,1,0:T(8,128)}) custom-call(f32[16,32,128]{2,1,0:T(8,128)} %r_hbm.1, f32[16,32,128]{2,1,0:T(8,128)} %kz_hbm.1, f32[16,32,128]{2,1,0:T(8,128)} %ky_hbm.1, f32[16,32,128]{2,1,0:T(8,128)} %kx_hbm.1, ...), custom_call_target="tpu_custom_call" | custom-call | tf_op jit(solution)/shard_map/pallas_call | solution.py:571
  18.9 3.3 %shard_map.104 = (f32[27,8,16,64]{3,2,1,0:T(8,128)}, f32[27,4,8,32]{3,2,1,0:T(8,128)}, f32[27,2,16,64]{3,2,1,0:T(8,128)}) custom-call(f32[17,40,128]{2,1,0:T(8,128)} %get-tuple-element.8.t1_hbm, f32[9,24,128]{2,1,0:T(8,128)} %get-tuple-element.9.t2_hbm, f32[64,128]{1,0:T(8,128)} %get-tuple-element.10.own_hbm, f32[320,128]{1,0:T(8,128)} %get-tuple-element.11.rb_hbm, ...), custom_call_target="tpu_custom_call" | custom-call | tf_op jit(solution)/shard_map/pallas_call | solution.py:591

commit v5 on v4

--- a/solution.py
+++ b/solution.py
@@ -175,7 +175,7 @@
         first, second = weights_y(level, 32, rows, last_y)
         y[row:row + rows, lane:lane + 128] = first
         y[row:row + rows, lane + 128:lane + 192] = second
-    return x.astype(ml_dtypes.bfloat16), y.astype(ml_dtypes.bfloat16)
+    return np.concatenate([x, y], axis=0).astype(ml_dtypes.bfloat16)
 
 
 S_PX, S_YD, S_YU, S_ROWS = 0, 64, 144, 192
@@ -184,10 +184,10 @@
 
 
 def main_kernel(
-    r_hbm, kz_hbm, ky_hbm, kx_hbm, wx_hbm, wy_hbm,
-    t1, t2, own, rb, g3,
-    f4, wx, wy, zs, zr,
-    gaf, gbf, ga1, gb1, ga2, gb2, ga3, gb3, c1, c2, c3, sb, p3,
+    r_hbm, kz_hbm, ky_hbm, kx_hbm, w_hbm,
+    t1a, t1b, t2, own, rb, g3,
+    f4, wx, wy, rims, rimr, zs, zr,
+    gaf, gbf, ga1, gb1, ga2, gb2, ga3, gb3, c3, sb, p3,
     lsem, send, recv, gsend, grecv,
 ):
     gz, gy, gx = lax.axis_index("gz"), lax.axis_index("gy"), lax.axis_index("gx")
@@ -211,8 +211,8 @@
         pltpu.make_async_copy(f, f4.at[j], lsem.at[j])
         for j, f in enumerate((r_hbm, kz_hbm, ky_hbm, kx_hbm))
     ]
-    loads.append(pltpu.make_async_copy(wx_hbm.at[end_x], wx, lsem.at[4]))
-    loads.append(pltpu.make_async_copy(wy_hbm.at[end_y], wy, lsem.at[5]))
+    loads.append(pltpu.make_async_copy(w_hbm.at[end_x, pl.ds(0, 512)], wx, lsem.at[4]))
+    loads.append(pltpu.make_async_copy(w_hbm.at[end_y, pl.ds(512, 64)], wy, lsem.at[5]))
     for c in loads:
         c.start()
 
@@ -300,9 +300,14 @@
         rest = jnp.concatenate([out2[two], out3[three]], axis=0)
         rest = jnp.where(low_pair, roll(side1[one], 65), rest)
         zs[start + Z_TWO:start + Z_ROWS] = jnp.where(high_one, roll(side1[one], 5), rest)
+        rims[16 * k:16 * k + 16] = out3[three]
     for j in range(5):
         c3[j] = out3[j]
     pl.semaphore_wait(barrier, slab - 1 + len(others))
+    round_z = [
+        copy(rims.at[0:32], rimr.at[0:32], (zm, gy, gx)),
+        copy(rims.at[32:48], rimr.at[32:48], (zp, gy, gx)),
+    ]
     faces = [
         copy(zs.at[pl.ds(0, 2 * Z_ROWS)], zr.at[pl.ds(0, 2 * Z_ROWS)], (zm, gy, gx)),
         copy(zs.at[pl.ds(2 * Z_ROWS, Z_ROWS)], zr.at[pl.ds(2 * Z_ROWS, Z_ROWS)], (zp, gy, gx)),
@@ -314,12 +319,15 @@
 
     def pack(k, one, side, two):
         if one is not None:
-            c1[k] = one
+            if k < 9:
+                t1a[k] = one
+            else:
+                t1b[k - 9] = one
             totals[0] = plus_of(totals[0], roll(side, k) if k else side)
             for start, row in ((S_YD, 21), (S_YD + 32, 23), (S_YU + 16, 22)):
                 sb[start + k:start + k + 1] = one[row:row + 1]
         if two is not None:
-            c2[k] = two
+            t2[k] = two
             totals[1] = plus_of(
                 totals[1], roll(jnp.where(lane2 >= 64, two, 0.0), 64 + k)
             )
@@ -336,16 +344,13 @@
         if k not in (0, 3, 4, 8):
             pack(k, None, None, out2[k])
 
-    for c in faces:
+    for c in round_z:
         c.wait_recv()
-
-    def came(k, start, rows):
-        value = zr[Z_ROWS * k + start:Z_ROWS * k + start + rows]
-        return jnp.where(low_z if k == 2 else top_z, 0.0, value)
-
-    lane3 = lax.broadcasted_iota(jnp.int32, (16, 128), 1)
-    down0, down1, low = (jnp.where(lane3 < 40, came(k, Z_THREE, 16), 0.0) for k in range(3))
-    fix3 = {0: low, 1: down0, 2: -low, 4: down1}
+    low = jnp.where(low_z, 0.0, rimr[32:48])
+    fix3 = {
+        0: low, 1: jnp.where(top_z, 0.0, rimr[0:16]),
+        2: -low, 4: jnp.where(top_z, 0.0, rimr[16:32]),
+    }
     packed = [None, None]
     for j in range(5):
         value = c3[j] if j not in fix3 else c3[j] + fix3[j]
@@ -362,8 +367,14 @@
         )
         c.start()
         gather.append(c)
-    mine = pltpu.make_async_copy(p3, g3.at[me], lsem.at[3])
-    mine.start()
+    g3[pl.ds(me, 1)] = p3[...][None]
+
+    for c in faces:
+        c.wait_recv()
+
+    def came(k, start, rows):
+        value = zr[Z_ROWS * k + start:Z_ROWS * k + start + rows]
+        return jnp.where(low_z if k == 2 else top_z, 0.0, value)
 
     def came_side(k):
         value = came(k, Z_TWO, 40)
@@ -407,17 +418,8 @@
     copy(sb.at[pl.ds(S_YD, 80)], rb.at[pl.ds(R_YD, 80)], (gz, ym, gx))
     copy(sb.at[pl.ds(S_YU, 48)], rb.at[pl.ds(R_YU, 48)], (gz, yp, gx))
 
-    stores = [
-        pltpu.make_async_copy(c1, t1, lsem.at[0]),
-        pltpu.make_async_copy(c2, t2, lsem.at[1]),
-        pltpu.make_async_copy(sb.at[pl.ds(S_PX, 64)], own, lsem.at[2]),
-    ]
-    for c in stores:
-        c.start()
-    for c in stores:
-        c.wait()
-    mine.wait()
-    for c in started[2:]:
+    own[...] = sb[S_PX:S_PX + 64]
+    for c in started[4:]:
         c.wait_recv()
     for c in gather:
         c.wait()
@@ -426,28 +428,23 @@
 
 
 def finish_kernel(
-    t1_hbm, t2_hbm, own_hbm, rb_hbm, g3_hbm, qx_hbm, qy_hbm, o1, o2, o3,
-    t1, t2, px, rb, g3, qx, qy, x1, x2, q3, s3, v1, v2, v3, csem, osem,
+    t1a, t1b, t2_in, own, rb, g3, q_hbm, o1, o2, o3,
+    t1, t2, px, q, x1, x2, q3, s3, v1, v2, v3, csem, osem,
 ):
     gy, gx = lax.axis_index("gy"), lax.axis_index("gx")
     ny, nx = lax.axis_size("gy"), lax.axis_size("gx")
-    loads = [
-        pltpu.make_async_copy(src, dst, csem.at[k])
-        for k, (src, dst) in enumerate((
-            (rb_hbm, rb), (t1_hbm, t1), (t2_hbm, t2), (own_hbm, px.at[0]),
-            (g3_hbm, g3), (qx_hbm, qx), (qy_hbm, qy),
-        ))
-    ]
-    for c in loads:
-        c.start()
+    load = pltpu.make_async_copy(q_hbm, q, csem.at[0])
+    load.start()
+    t1[0:9] = t1a[...]
+    t1[9:17] = t1b[...]
+    t2[...] = t2_in[...]
+    px[0] = own[...]
 
     def present(flag):
         return jnp.where(flag, 1.0, 0.0).astype(F32)
 
     from_up_y, from_low_y = present(gy < ny - 1), present(gy > 0)
     from_up_x, from_low_x = present(gx < nx - 1), present(gx > 0)
-    for c in loads[0:4]:
-        c.wait()
 
     for k in range(2):
         px[1 + k] = rb[R_X + 64 * k:R_X + 64 * k + 64]
@@ -526,10 +523,9 @@
     expand(t1, x1, v1, o1, 8, 16, 64)
     expand(t2, x2, v2, o2, 4, 8, 32)
 
-    for c in loads[4:]:
-        c.wait()
+    load.wait()
     blocks = jnp.concatenate(split(g3[...].reshape(384, 128)), axis=1)
-    spread = dot(blocks, qx[...])
+    spread = dot(blocks, q[0:256])
     lane = lax.broadcasted_iota(jnp.int32, (24, 128), 1)
     for by in range(4):
         for layer in range(3):
@@ -547,7 +543,7 @@
         rows = jnp.concatenate(
             [q3[24 * by + 8 * h:24 * by + 8 * h + 16, :] for by in range(4)], axis=0
         )
-        placed = dot(qy[h], jnp.concatenate(split(rows), axis=0))
+        placed = dot(q[256 + 48 * h:304 + 48 * h, 0:128], jnp.concatenate(split(rows), axis=0))
         for j in range(3):
             if 3 * h + j < 5:
                 s3[3 * h + j] = placed[0:40, 128 * j:128 * j + 128]
@@ -558,53 +554,58 @@
 
 def shards(coeff_z, coeff_y, coeff_x, reaction):
     hbm = pl.BlockSpec(memory_space=pltpu.HBM)
+    vmem = pl.BlockSpec(memory_space=pltpu.VMEM)
     shape = jax.ShapeDtypeStruct
     v = pltpu.VMEM
     dma = pltpu.SemaphoreType.DMA
-    pairs = [all_weights(flag, flag) for flag in (False, True)]
-    wx, wy = (jnp.asarray(np.stack([pair[k] for pair in pairs])) for k in range(2))
+    weights = jnp.asarray(np.stack([all_weights(flag, flag) for flag in (False, True)]))
     between = (
-        shape((17, 40, 128), F32), shape((9, 24, 128), F32), shape((64, 128), F32),
+        shape((9, 40, 128), F32), shape((8, 40, 128), F32), shape((9, 24, 128), F32),
+        shape((64, 128), F32),
         shape((R_ROWS, 128), F32), shape((16, 24, 128), F32),
     )
-    place = jnp.asarray(np.stack([place_y(4, 4, 48, 16, shift) for shift in (0, 4)]))
+    place_rows = np.concatenate([place_y(4, 4, 48, 16, shift) for shift in (0, 4)], axis=0)
+    place_rows = np.pad(place_rows.astype(np.float32), ((0, 0), (0, 256)))
+    place = jnp.asarray(
+        np.concatenate([place_x(16).astype(np.float32), place_rows]).astype(ml_dtypes.bfloat16)
+    )
     middle = pl.pallas_call(
         main_kernel,
         out_shape=between,
-        in_specs=[hbm] * 6,
-        out_specs=(hbm,) * 5,
+        in_specs=[hbm] * 5,
+        out_specs=(vmem,) * 6,
         scratch_shapes=[
             v((4, 16, 32, 128), F32), v((512, 512), BF16), v((64, 512), BF16),
+            v((48, 128), F32), v((48, 128), F32),
             v((3 * Z_ROWS, 128), F32), v((3 * Z_ROWS, 128), F32),
             v((128, 3 * 128), BF16), v((64, 3 * 128), BF16),
             v((128, 16 * 128), BF16), v((64, 16 * 128), BF16),
             v((128, 11 * 128), BF16), v((64, 11 * 128), BF16),
             v((128, 7 * 128), BF16), v((64, 7 * 128), BF16),
-            v((17, 40, 128), F32), v((9, 24, 128), F32), v((5, 16, 128), F32),
+            v((5, 16, 128), F32),
             v((S_ROWS, 128), F32), v((24, 128), F32),
-            dma((6,)), dma((10,)), dma((10,)), dma((15,)), dma((15,)),
+            dma((6,)), dma((12,)), dma((12,)), dma((15,)), dma((15,)),
         ],
         compiler_params=pltpu.CompilerParams(
-            collective_id=0, has_side_effects=True, vmem_limit_bytes=62 << 20
+            collective_id=0, has_side_effects=True, vmem_limit_bytes=53 << 20
         ),
-    )(reaction, coeff_z, coeff_y, coeff_x, wx, wy)
+    )(reaction, coeff_z, coeff_y, coeff_x, weights)
     return pl.pallas_call(
         finish_kernel,
         out_shape=(
             shape((27, 8, 16, 64), F32), shape((27, 4, 8, 32), F32), shape((27, 2, 16, 64), F32),
         ),
-        in_specs=[hbm] * 7,
+        in_specs=[vmem] * 6 + [hbm],
         out_specs=(hbm,) * 3,
         scratch_shapes=[
             v((17, 40, 128), F32), v((9, 24, 128), F32), v((3, 64, 128), F32),
-            v((R_ROWS, 128), F32), v((16, 24, 128), F32),
-            v((256, 384), BF16), v((2, 48, 128), BF16), v((40, 128), F32), v((24, 128), F32),
+            v((352, 384), BF16), v((40, 128), F32), v((24, 128), F32),
             v((96, 384), F32), v((5, 40, 128), F32),
             v((27, 8, 16, 64), F32), v((27, 4, 8, 32), F32), v((27, 2, 16, 64), F32),
-            dma((7,)), dma((9,)),
+            dma((1,)), dma((9,)),
         ],
-        compiler_params=pltpu.CompilerParams(vmem_limit_bytes=62 << 20),
-    )(*middle, jnp.asarray(place_x(16)), place)
+        compiler_params=pltpu.CompilerParams(vmem_limit_bytes=53 << 20),
+    )(*middle, place)
 
 
 def solution(mesh):

time: 22.3 us -> 21.7 us (0.973)
  Pallas kernels: 21.5 us -> 20.9 us
    pallas_call x1, Pallas kernels: 18.2 us -> 17.8 us  [shards(): pl.pallas_call(main_kernel, out_shape=between, in_specs=[hbm] * 5, out_sp...]
where the time goes in v5:
time: 21.7 us; the launch traced here: 21.5 us
  Pallas kernels  20.9 us (96%)
  between operations  0.64 us (3%)
    pallas_call x1, Pallas kernels, shards(): pl.pallas_call(main_kernel, out_shape=between, in_specs=[hbm] * 5, out_sp...  17.8 us
    pallas_call x1, Pallas kernels, shards(): pl.pallas_call(finish_kernel, out_shape=(shape((27, 8, 16, 64), F32), sha...  3.08 us

profile of v5, /device:TPU:1, one launch (start us, length us, event | category | flops | bytes accessed | tf_op | source)
XLA Modules:
  0.0 21.5 jit_solution(1254322856350872191)
XLA Ops:
  0.6 17.8 %shard_map.85 = (f32[9,40,128]{2,1,0:T(8,128)S(1)}, f32[8,40,128]{2,1,0:T(8,128)S(1)}, f32[9,24,128]{2,1,0:T(8,128)S(1)}, f32[64,128]{1,0:T(8,128)S(1)}, f32[320...) custom-call(f32[16,32,128]{2,1,0:T(8,128)} %r_hbm.1, f32[16,32,128]{2,1,0:T(8,128)} %kz_hbm.1, f32[16,32,128]{2,1,0:T(8,128)} %ky_hbm.1, ...), custom_call_target="tpu_custom_call" | custom-call | tf_op jit(solution)/shard_map/pallas_call | solution.py:572
  18.5 3.1 %shard_map.86 = (f32[27,8,16,64]{3,2,1,0:T(8,128)}, f32[27,4,8,32]{3,2,1,0:T(8,128)}, f32[27,2,16,64]{3,2,1,0:T(8,128)}) custom-call(f32[9,40,128]{2,1,0:T(8,128)S(1)} %get-tuple-element.9.t1a, f32[8,40,128]{2,1,0:T(8,128)S(1)} %get-tuple-element.10.t1b, f32[9,24,128]{2,1,0:T(8,128)S(1)} %get-tuple-element.11.t2_in, f32[64,128]{1,0:T(8,128)S(1)} %get-tuple-element.12.own, ...), custom_call_target="tpu_custom_call" | custom-call | tf_op jit(solution)/shard_map/pallas_call | solution.py:593

commit v6 on v5

--- a/solution.py
+++ b/solution.py
@@ -88,11 +88,11 @@
 
 
 def place_x(count):
-    out = np.zeros((2, 128, 3 * 128))
+    out = np.zeros((128, 3 * 128))
     for layer in range(3):
         for lane, (plus, index) in enumerate(lanes_of(3, count * 8)[0]):
-            out[:, 40 * layer + lane, layer * 128 + plus * 64 + count + index] = 1.0
-    return out.reshape(256, 384).astype(ml_dtypes.bfloat16)
+            out[40 * layer + lane, layer * 128 + plus * 64 + count + index] = 1.0
+    return out.astype(ml_dtypes.bfloat16)
 
 
 def place_y(blocks, count, rows, packed, shift):
@@ -175,7 +175,10 @@
         first, second = weights_y(level, 32, rows, last_y)
         y[row:row + rows, lane:lane + 128] = first
         y[row:row + rows, lane + 128:lane + 192] = second
-    return np.concatenate([x, y], axis=0).astype(ml_dtypes.bfloat16)
+    place = np.zeros((128, 512))
+    place[:, 0:384] = place_x(16)
+    place[0:96, 384:512] = np.concatenate([place_y(4, 4, 48, 16, shift) for shift in (0, 4)])
+    return np.concatenate([x, y, place], axis=0).astype(ml_dtypes.bfloat16)
 
 
 S_PX, S_YD, S_YU, S_ROWS = 0, 64, 144, 192
@@ -185,7 +188,7 @@
 
 def main_kernel(
     r_hbm, kz_hbm, ky_hbm, kx_hbm, w_hbm,
-    t1a, t1b, t2, own, rb, g3,
+    t1a, t1b, t2, own, rb, g3, q1, q2,
     f4, wx, wy, rims, rimr, zs, zr,
     gaf, gbf, ga1, gb1, ga2, gb2, ga3, gb3, c3, sb, p3,
     lsem, send, recv, gsend, grecv,
@@ -213,7 +216,11 @@
     ]
     loads.append(pltpu.make_async_copy(w_hbm.at[end_x, pl.ds(0, 512)], wx, lsem.at[4]))
     loads.append(pltpu.make_async_copy(w_hbm.at[end_y, pl.ds(512, 64)], wy, lsem.at[5]))
-    for c in loads:
+    later = [
+        pltpu.make_async_copy(w_hbm.at[0, pl.ds(576, 128), pl.ds(0, 384)], q1, lsem.at[6]),
+        pltpu.make_async_copy(w_hbm.at[0, pl.ds(576, 96), pl.ds(384, 128)], q2, lsem.at[7]),
+    ]
+    for c in loads + later:
         c.start()
 
     started = []
@@ -421,24 +428,21 @@
     own[...] = sb[S_PX:S_PX + 64]
     for c in started[4:]:
         c.wait_recv()
-    for c in gather:
+    for c in gather + later:
         c.wait()
     for c in started:
         c.wait_send()
 
 
 def finish_kernel(
-    t1a, t1b, t2_in, own, rb, g3, q_hbm, o1, o2, o3,
-    t1, t2, px, q, x1, x2, q3, s3, v1, v2, v3, csem, osem,
+    t1a, t1b, t2_in, own, rb, g3, q1, q2, o1, o2, o3,
+    t1, t2, x1, x2, q3, s3, v1, v2, v3, osem,
 ):
     gy, gx = lax.axis_index("gy"), lax.axis_index("gx")
     ny, nx = lax.axis_size("gy"), lax.axis_size("gx")
-    load = pltpu.make_async_copy(q_hbm, q, csem.at[0])
-    load.start()
     t1[0:9] = t1a[...]
     t1[9:17] = t1b[...]
     t2[...] = t2_in[...]
-    px[0] = own[...]
 
     def present(flag):
         return jnp.where(flag, 1.0, 0.0).astype(F32)
@@ -446,29 +450,44 @@
     from_up_y, from_low_y = present(gy < ny - 1), present(gy > 0)
     from_up_x, from_low_x = present(gx < nx - 1), present(gx > 0)
 
-    for k in range(2):
-        px[1 + k] = rb[R_X + 64 * k:R_X + 64 * k + 64]
-    side = [(rb[R_YD + 64:R_YD + 80], rb[R_YU:R_YU + 16])]
+    row8 = lax.broadcasted_iota(jnp.int32, (8, 128), 0)
+    first_row, last_row = row8 == 0, row8 == 7
+
+    def at_row(where, group, value):
+        return group + jnp.where(where, value, 0.0)
+
+    def y_fixed(same, rim, plus, same_up, plus_up, low):
+        same[-1] = at_row(last_row, same[-1], same_up)
+        same[0] = at_row(first_row, same[0], low)
+        plus[-1] = at_row(last_row, plus[-1], plus_up)
+        rim = jnp.where(last_row, (rim - low) * from_low_y, rim)
+        return jnp.concatenate(same + [rim] + plus, axis=0)
+
+    sides = [(own, 0, rb[R_YD + 64:R_YD + 80], rb[R_YU:R_YU + 16])]
     for xi in range(2):
-        side.append(tuple(rb[R_D + 16 * k:R_D + 16 * k + 16] for k in (xi, 2 + xi)))
-    for k, (upper, lower) in enumerate(side):
+        sides.append((
+            rb, R_X + 64 * xi, rb[R_D + 16 * xi:R_D + 16 * xi + 16],
+            rb[R_D + 32 + 16 * xi:R_D + 48 + 16 * xi],
+        ))
+    columns = [[], []]
+    for ref, start, upper, lower in sides:
         upper, lower = from_up_y * upper, from_low_y * lower
-        for same, plus, rim, group in ((0, 16, 48, 0), (32, 40, 56, 8)):
-            n = plus - same
-            for row, value in (
-                (same + n - 1, upper[group + 5:group + 6]),
-                (plus + n - 1, upper[group + 7:group + 8]),
-                (same, lower[group + 6:group + 7]),
-            ):
-                px[k, row:row + 1] = px[k, row:row + 1] + value
-            row = rim + 7
-            px[k, row:row + 1] = (px[k, row:row + 1] - lower[group + 6:group + 7]) * from_low_y
+        for level, (same, plus, rim, size) in enumerate(((0, 16, 48, 16), (32, 40, 56, 8))):
+            groups = [
+                [ref[start + at + 8 * k:start + at + 8 * k + 8] for k in range(size // 8)]
+                for at in (same, plus)
+            ]
+            up, low = upper[8 * level:8 * level + 8], lower[8 * level:8 * level + 8]
+            columns[level].append(y_fixed(
+                groups[0], ref[start + rim:start + rim + 8], groups[1],
+                up[5:6], up[7:8], low[6:7],
+            ))
 
     sets = (
-        (t1, x1, 8, 16, 64, (0, 16, 48), 0),
-        (t2, x2, 4, 8, 32, (32, 40, 56), 17),
+        (0, t1, x1, 8, 16, 64, 0),
+        (1, t2, x2, 4, 8, 32, 17),
     )
-    for t, x, lz, n, lanes, parts, rows_at in sets:
+    for level, t, x, lz, n, lanes, rows_at in sets:
         count = 2 * lz + 1
         same_up = from_up_y * rb[R_YD + rows_at:R_YD + rows_at + count]
         plus_up = from_up_y * rb[R_YD + 32 + rows_at:R_YD + 32 + rows_at + count]
@@ -479,12 +498,9 @@
             t[j, 0:1] = t[j, 0:1] + low[j:j + 1]
             t[j, n + 7:n + 8] = (t[j, n + 7:n + 8] - low[j:j + 1]) * from_low_y
 
-        def column(k):
-            same, plus, rim = (px[k, s:s + z] for s, z in zip(parts, (n, n, 8)))
-            return jnp.concatenate([same, rim, plus], axis=0)
-
-        above, below = from_up_x * column(1), from_low_x * column(2)
-        x[...] = (column(0) - roll(below, lanes // 2)) * from_low_x
+        own_column, above, below = columns[level]
+        above, below = from_up_x * above, from_low_x * below
+        x[...] = (own_column - roll(below, lanes // 2)) * from_low_x
         lane = lax.broadcasted_iota(jnp.int32, above.shape, 1)
         at_end = (lane == lanes - 1) | (lane == 2 * lanes - 1)
         for j in range(count):
@@ -523,9 +539,8 @@
     expand(t1, x1, v1, o1, 8, 16, 64)
     expand(t2, x2, v2, o2, 4, 8, 32)
 
-    load.wait()
-    blocks = jnp.concatenate(split(g3[...].reshape(384, 128)), axis=1)
-    spread = dot(blocks, q[0:256])
+    high, low = split(g3[...].reshape(384, 128))
+    spread = dot(high, q1[...]) + dot(low, q1[...])
     lane = lax.broadcasted_iota(jnp.int32, (24, 128), 1)
     for by in range(4):
         for layer in range(3):
@@ -543,7 +558,7 @@
         rows = jnp.concatenate(
             [q3[24 * by + 8 * h:24 * by + 8 * h + 16, :] for by in range(4)], axis=0
         )
-        placed = dot(q[256 + 48 * h:304 + 48 * h, 0:128], jnp.concatenate(split(rows), axis=0))
+        placed = dot(q2[48 * h:48 * h + 48], jnp.concatenate(split(rows), axis=0))
         for j in range(3):
             if 3 * h + j < 5:
                 s3[3 * h + j] = placed[0:40, 128 * j:128 * j + 128]
@@ -563,17 +578,13 @@
         shape((9, 40, 128), F32), shape((8, 40, 128), F32), shape((9, 24, 128), F32),
         shape((64, 128), F32),
         shape((R_ROWS, 128), F32), shape((16, 24, 128), F32),
-    )
-    place_rows = np.concatenate([place_y(4, 4, 48, 16, shift) for shift in (0, 4)], axis=0)
-    place_rows = np.pad(place_rows.astype(np.float32), ((0, 0), (0, 256)))
-    place = jnp.asarray(
-        np.concatenate([place_x(16).astype(np.float32), place_rows]).astype(ml_dtypes.bfloat16)
+        shape((128, 384), BF16), shape((96, 128), BF16),
     )
     middle = pl.pallas_call(
         main_kernel,
         out_shape=between,
         in_specs=[hbm] * 5,
-        out_specs=(vmem,) * 6,
+        out_specs=(vmem,) * 8,
         scratch_shapes=[
             v((4, 16, 32, 128), F32), v((512, 512), BF16), v((64, 512), BF16),
             v((48, 128), F32), v((48, 128), F32),
@@ -584,10 +595,10 @@
             v((128, 7 * 128), BF16), v((64, 7 * 128), BF16),
             v((5, 16, 128), F32),
             v((S_ROWS, 128), F32), v((24, 128), F32),
-            dma((6,)), dma((12,)), dma((12,)), dma((15,)), dma((15,)),
+            dma((8,)), dma((12,)), dma((12,)), dma((15,)), dma((15,)),
         ],
         compiler_params=pltpu.CompilerParams(
-            collective_id=0, has_side_effects=True, vmem_limit_bytes=53 << 20
+            collective_id=0, has_side_effects=True, vmem_limit_bytes=(52 << 20) + 921600
         ),
     )(reaction, coeff_z, coeff_y, coeff_x, weights)
     return pl.pallas_call(
@@ -595,17 +606,17 @@
         out_shape=(
             shape((27, 8, 16, 64), F32), shape((27, 4, 8, 32), F32), shape((27, 2, 16, 64), F32),
         ),
-        in_specs=[vmem] * 6 + [hbm],
+        in_specs=[vmem] * 8,
         out_specs=(hbm,) * 3,
         scratch_shapes=[
-            v((17, 40, 128), F32), v((9, 24, 128), F32), v((3, 64, 128), F32),
-            v((352, 384), BF16), v((40, 128), F32), v((24, 128), F32),
+            v((17, 40, 128), F32), v((9, 24, 128), F32),
+            v((40, 128), F32), v((24, 128), F32),
             v((96, 384), F32), v((5, 40, 128), F32),
             v((27, 8, 16, 64), F32), v((27, 4, 8, 32), F32), v((27, 2, 16, 64), F32),
-            dma((1,)), dma((9,)),
+            dma((9,)),
         ],
-        compiler_params=pltpu.CompilerParams(vmem_limit_bytes=53 << 20),
-    )(*middle, place)
+        compiler_params=pltpu.CompilerParams(vmem_limit_bytes=(52 << 20) + 921600),
+    )(*middle)
 
 
 def solution(mesh):

time: 21.7 us -> 20.7 us (0.954)
  Pallas kernels: 20.9 us -> 19.9 us
    pallas_call x1, Pallas kernels: 3.08 us -> 2.09 us  [shards(): pl.pallas_call(finish_kernel, out_shape=(shape((27, 8, 16, 64), F32), sha...]
where the time goes in v6:
time: 20.7 us; the launch traced here: 20.6 us
  Pallas kernels  19.9 us (96%)
  between operations  0.64 us (3%)
    pallas_call x1, Pallas kernels, shards(): pl.pallas_call(main_kernel, out_shape=between, in_specs=[hbm] * 5, out_sp...  17.9 us
    pallas_call x1, Pallas kernels, shards(): pl.pallas_call(finish_kernel, out_shape=(shape((27, 8, 16, 64), F32), sha...  2.09 us

profile of v6, /device:TPU:1, one launch (start us, length us, event | category | flops | bytes accessed | tf_op | source)
XLA Modules:
  0.0 20.6 jit_solution(15113980963985879918)
XLA Ops:
  0.6 17.9 %shard_map.76 = (f32[9,40,128]{2,1,0:T(8,128)S(1)}, f32[8,40,128]{2,1,0:T(8,128)S(1)}, f32[9,24,128]{2,1,0:T(8,128)S(1)}, f32[64,128]{1,0:T(8,128)S(1)}, f32[320...) custom-call(f32[16,32,128]{2,1,0:T(8,128)} %r_hbm.1, ...), custom_call_target="tpu_custom_call" | custom-call | tf_op jit(solution)/shard_map/pallas_call | solution.py:583
  18.5 2.1 %shard_map.77 = (f32[27,8,16,64]{3,2,1,0:T(8,128)}, f32[27,4,8,32]{3,2,1,0:T(8,128)}, f32[27,2,16,64]{3,2,1,0:T(8,128)}) custom-call(f32[9,40,128]{2,1,0:T(8,128)S(1)} %get-tuple-element.11.t1a, f32[8,40,128]{2,1,0:T(8,128)S(1)} %get-tuple-element.12.t1b, f32[9,24,128]{2,1,0:T(8,128)S(1)} %get-tuple-element.13.t2_in, f32[64,128]{1,0:T(8,128)S(1)} %get-tuple-element.14.own, ...), custom_call_target="tpu_custom_call" | custom-call | tf_op jit(solution)/shard_map/pallas_call | solution.py:604

commit v7 on v6

--- a/solution.py
+++ b/solution.py
@@ -510,7 +510,7 @@
     pending = []
 
     def expand(t, x, v, o, nz, ny, n):
-        done = [set() for _ in range(3)]
+        done, step = [0, 0, 0], min(nz, 4)
         rows = {0: slice(ny + 7, 2 * ny + 7), 1: slice(0, ny), 2: slice(ny + 8, 2 * ny + 8)}
         for k in range(2 * nz + 1):
             value = t[k]
@@ -528,11 +528,13 @@
                 for a, layer in targets:
                     for b in range(3):
                         v[9 * a + 3 * b + c, layer] = plane[rows[b]]
-            for a, layer in targets:
-                done[a].add(layer)
-                if len(done[a]) == nz:
-                    part = pl.ds(9 * a, 9)
-                    copy = pltpu.make_async_copy(v.at[part], o.at[part], osem.at[len(pending)])
+            for a, _ in targets:
+                done[a] += 1
+                if done[a] % step == 0:
+                    part, depth = pl.ds(9 * a, 9), pl.ds(done[a] - step, step)
+                    copy = pltpu.make_async_copy(
+                        v.at[part, depth], o.at[part, depth], osem.at[len(pending)]
+                    )
                     copy.start()
                     pending.append(copy)
 
@@ -613,7 +615,7 @@
             v((40, 128), F32), v((24, 128), F32),
             v((96, 384), F32), v((5, 40, 128), F32),
             v((27, 8, 16, 64), F32), v((27, 4, 8, 32), F32), v((27, 2, 16, 64), F32),
-            dma((9,)),
+            dma((12,)),
         ],
         compiler_params=pltpu.CompilerParams(vmem_limit_bytes=(52 << 20) + 921600),
     )(*middle)

time: 20.7 us -> 20.7 us (level)
  no operation moved by 1% of the time
where the time goes in v7:
time: 20.7 us; the launch traced here: 20.5 us
  Pallas kernels  19.9 us (96%)
  between operations  0.64 us (3%)
    pallas_call x1, Pallas kernels, shards(): pl.pallas_call(main_kernel, out_shape=between, in_specs=[hbm] * 5, out_sp...  17.9 us
    pallas_call x1, Pallas kernels, shards(): pl.pallas_call(finish_kernel, out_shape=(shape((27, 8, 16, 64), F32), sha...  2.05 us

profile of v7, /device:TPU:1, one launch (start us, length us, event | category | flops | bytes accessed | tf_op | source)
XLA Modules:
  0.0 20.5 jit_solution(6838355971292669721)
XLA Ops:
  0.6 17.9 %shard_map.76 = (f32[9,40,128]{2,1,0:T(8,128)S(1)}, f32[8,40,128]{2,1,0:T(8,128)S(1)}, f32[9,24,128]{2,1,0:T(8,128)S(1)}, f32[64,128]{1,0:T(8,128)S(1)}, f32[320...) custom-call(f32[16,32,128]{2,1,0:T(8,128)} %r_hbm.1, ...), custom_call_target="tpu_custom_call" | custom-call | tf_op jit(solution)/shard_map/pallas_call | solution.py:585
  18.5 2.1 %shard_map.77 = (f32[27,8,16,64]{3,2,1,0:T(8,128)}, f32[27,4,8,32]{3,2,1,0:T(8,128)}, f32[27,2,16,64]{3,2,1,0:T(8,128)}) custom-call(f32[9,40,128]{2,1,0:T(8,128)S(1)} %get-tuple-element.11.t1a, f32[8,40,128]{2,1,0:T(8,128)S(1)} %get-tuple-element.12.t1b, f32[9,24,128]{2,1,0:T(8,128)S(1)} %get-tuple-element.13.t2_in, f32[64,128]{1,0:T(8,128)S(1)} %get-tuple-element.14.own, ...), custom_call_target="tpu_custom_call" | custom-call | tf_op jit(solution)/shard_map/pallas_call | solution.py:606
